TPU v7x, 32 devices: a whole 2x2x4 slice. The times are simulated.
32 devices in a mesh: groups: 2 (over x), tile: 8 (over z, y), tm: 2 (over core).
Axes of the slice: x: 2, y: 2, z: 4, core: 2. Of those that a mesh axis runs over, the one named last changes fastest.
Arguments:
- pixels: bfloat16 [64, 3, 64, 1280], P(('groups', 'tile', 'tm')), parts along dimension 0, may hold values from -1 to 1
- owner: int32 [32], P('groups'), parts along dimension 0, may hold values from 0 to 15, as said below
- patch_weight: bfloat16 [768, 1024], replicated, may hold values from -0.21875 to 0.21875
- norm_gain: float32 [1024], replicated, may hold values from 0.25 to 1.75
- qkv_weight: bfloat16 [1024, 3072], replicated, may hold values from -0.1875 to 0.1875
- out_weight: bfloat16 [1024, 1024], replicated, may hold values from -0.1875 to 0.1875
- post_gain: float32 [1024], replicated, may hold values from 0.25 to 1.75
- text_embed: float32 [2048], P('groups'), parts along dimension 0, may hold values from -6 to 6
- conv_out_weight: bfloat16 [3, 3, 128, 3], replicated, may hold values from -1.25 to 1.25
- conv_weight: bfloat16 [3, 3, 128, 128], replicated, may hold values from -0.1875 to 0.1875
- activations: bfloat16 [32, 64, 1280, 128], P(('groups', 'tm'), None, 'tile'), parts along dimension 0, may hold values from -8 to 8
Outputs:
- input_grad: bfloat16 [32, 64, 1280, 128], P(('groups', 'tm'), None, 'tile'), parts along dimension 0
There are 2 independent parts, one for each index of `groups`. A program takes and returns all parts, laid end to end along the dimension named above; an argument that names none is the same for every part. Nothing has to cross between parts.
Inputs may be any that keep to these rules, and one draw needn't show every extreme that they name: Each owner holds at most 2 frames, and one owner holds exactly 2.
All inputs are finite; a program needn't handle non-finite values.
Results may differ from a plain program's by a relative error of at most 0.018.
Values may be sent and summed in bfloat16 or wider, within the bound.
No kernel may reach another device: no remote copies, remote signals or barrier semaphores. Data moves between devices by JAX's collectives and lax.ppermute only.
A program may use at most 192 MiB of HBM per device.

v0:
```python
import functools

import jax
import jax.numpy as jnp
from jax import lax
from jax.experimental import pallas as pl
from jax.experimental.pallas import tpu as pltpu
from jax.sharding import PartitionSpec as P

HEADS = 16
HEAD_DIM = 64
PATCH = 16
EPS = 1e-06
LOGIT_SCALE = 100.0
LOSS_SCALE = 64.0

LANES = 128
SUB = 16
NARROW = jnp.bfloat16
WIDE = jnp.float32


def silu_slope(pre_value):
    half = jnp.tanh(0.5 * pre_value)
    return 0.5 + 0.5 * half + (0.25 * pre_value) * (1.0 - half * half)


def decoder_kernel(
    height,
    width,
    block_rows,
    pick_ref,
    own_ref,
    near_ref,
    far_ref,
    left_ref,
    right_ref,
    act_ref,
    w_edge_ref,
    w_one_ref,
    w_two_ref,
    out_ref,
    taps_ref,
    row_ref,
    edge_ref,
    grads_ref,
):
    frame = pl.program_id(0)
    rem = max(width + 4 - LANES, 0)
    chunks = -(-width // LANES)

    @pl.when(frame == 0)
    def _():
        taps_ref[...] = jnp.zeros_like(taps_ref)
        for s in range(3):
            zero_row = jnp.zeros(grads_ref.shape[2:], grads_ref.dtype)
            grads_ref[s, 0] = zero_row
            grads_ref[s, height + 1] = zero_row

    is_near = own_ref[frame] != 0
    message = jnp.where(is_near, near_ref[0].astype(jnp.float32), far_ref[0].astype(jnp.float32))
    mains = [message[k * height : (k + 1) * height] for k in range(3)]
    if rem > 0:
        tail = message[3 * height : 4 * height]
    for k in range(3):
        if rem > 0:
            line = jnp.concatenate([mains[k], tail[:, k * rem : (k + 1) * rem]], axis=1)
        else:
            line = mains[k]
        for s in range(3):
            for c in range(chunks):
                start = 3 - s + c * LANES
                stop = min(start + LANES, width + 4)
                part = line[:, start:stop]
                if stop - start < LANES:
                    blank = jnp.zeros((height, LANES - (stop - start)), jnp.float32)
                    part = jnp.concatenate([part, blank], axis=1)
                taps_ref[c, pl.ds(SUB + 3 * s + k, height, stride=SUB), :] = part
    pieces = mains + ([tail] if rem > 0 else [])
    wide = jnp.concatenate(pieces, axis=1).astype(jnp.bfloat16)
    per_tap = jnp.dot(wide, w_edge_ref[...], preferred_element_type=jnp.float32)
    zeros = jnp.zeros((1, 2 * LANES), jnp.float32)
    first, middle, last = (per_tap[:, i * 2 * LANES : (i + 1) * 2 * LANES] for i in range(3))
    edge = (
        jnp.concatenate([first[1:], zeros], axis=0)
        + middle
        + jnp.concatenate([zeros, last[: height - 1]], axis=0)
    )
    edge_ref[:, :LANES] = edge[:, :LANES] * silu_slope(left_ref[0].astype(jnp.float32))
    edge_ref[:, LANES:] = edge[:, LANES:] * silu_slope(right_ref[0].astype(jnp.float32))

    pairs = block_rows // 2

    def produce(block):
        base = block * block_rows
        lhs = jnp.concatenate(
            [
                taps_ref[c, (base + 2 * p) * SUB : (base + 2 * p + 4) * SUB, :]
                .T[: min(LANES, width - c * LANES)]
                .astype(jnp.bfloat16)
                for p in range(pairs)
                for c in range(chunks)
            ],
            axis=0,
        )
        back = jnp.dot(lhs, w_one_ref[...], preferred_element_type=jnp.float32)
        for i in range(block_rows):
            y = base + i
            p, h = i // 2, i % 2
            part = back[p * width : (p + 1) * width, h * LANES : (h + 1) * LANES]
            value = part * silu_slope(act_ref[0, y].astype(jnp.float32))
            slot = i % 4
            row_ref[slot, 8 : 8 + width, :] = value
            row_ref[slot, 7:8, :] = edge_ref[y : y + 1, :LANES]
            row_ref[slot, 8 + width : 9 + width, :] = edge_ref[y : y + 1, LANES:]
            grads_ref[0, y + 1] = row_ref[slot, 9 : 9 + width, :].astype(jnp.bfloat16)
            grads_ref[1, y + 1] = value.astype(jnp.bfloat16)
            grads_ref[2, y + 1] = row_ref[slot, 7 : 7 + width, :].astype(jnp.bfloat16)

    def consume(block):
        base = block * block_rows
        total = None
        slabs = []
        for j in range(4):
            for s in range(3):
                slabs.append(
                    jnp.concatenate([grads_ref[s, base + 2 * p + j] for p in range(pairs)], axis=0)
                )
        lhs = jnp.concatenate(slabs, axis=1)
        total = jnp.dot(lhs, w_two_ref[...], preferred_element_type=jnp.float32)
        for i in range(block_rows):
            p, h = i // 2, i % 2
            part = total[p * width : (p + 1) * width, h * LANES : (h + 1) * LANES]
            centre = grads_ref[1, base + i + 1].astype(jnp.float32)
            out_ref[0, base + i] = (part + centre).astype(out_ref.dtype)

    blocks = height // block_rows
    produce(0)
    for block in range(blocks):
        if block + 1 < blocks:
            produce(block + 1)
        consume(block)


def decoder_weights(conv_out_weight, conv_weight, height, width):
    rem = max(width + 4 - LANES, 0)
    taps_out = conv_out_weight.transpose(0, 1, 3, 2)
    channels = conv_weight.shape[2]
    small = jnp.pad(
        taps_out.reshape(3, 9, channels), ((0, 0), (0, SUB - 9), (0, 0))
    )
    none = jnp.zeros_like(small[0])
    w_one = jnp.concatenate(
        [
            jnp.stack([small[h - j + 2] if 0 <= h - j + 2 < 3 else none for j in range(4)])
            for h in range(2)
        ],
        axis=2,
    ).reshape(4 * SUB, 2 * channels)
    big = conv_weight.transpose(0, 1, 3, 2)
    none = jnp.zeros_like(big[0])
    w_two = jnp.concatenate(
        [
            jnp.stack([big[h - j + 2] if 0 <= h - j + 2 < 3 else none for j in range(4)])
            for h in range(2)
        ],
        axis=3,
    ).reshape(4 * 3 * channels, 2 * channels)
    flipped = taps_out[:, ::-1].transpose(0, 2, 1, 3)
    groups = 4 if rem > 0 else 3
    sides = []
    for r in range(3):
        left = jnp.zeros((groups * LANES, channels), conv_out_weight.dtype)
        right = jnp.zeros((groups * LANES, channels), conv_out_weight.dtype)
        for k in range(3):
            left = left.at[k * LANES : k * LANES + 3].set(flipped[r, k])
            for i in range(3):
                lane = width + 1 + i
                if lane < LANES:
                    place = k * LANES + lane
                else:
                    place = 3 * LANES + k * rem + lane - LANES
                right = right.at[place].set(flipped[r, k, i])
        sides.extend([left, right])
    w_edge = jnp.concatenate(sides, axis=1)
    return w_edge, w_one, w_two


def decode(pick, own, near, far, left, right, activations, conv_out_weight, conv_weight, block_rows):
    frames, height, width, channels = activations.shape
    rows = near.shape[1]
    w_edge, w_one, w_two = decoder_weights(conv_out_weight, conv_weight, height, width)
    whole = lambda shape: pl.BlockSpec(shape, lambda f, *_: (0,) * len(shape))
    padded = -(-(width + 9) // 8) * 8 + 8
    return pl.pallas_call(
        functools.partial(decoder_kernel, height, width, block_rows),
        out_shape=jax.ShapeDtypeStruct(activations.shape, jnp.bfloat16),
        grid_spec=pltpu.PrefetchScalarGridSpec(
            num_scalar_prefetch=2,
            grid=(frames,),
            in_specs=[
                pl.BlockSpec((1, rows, LANES), lambda f, pick, own: (pick[f], 0, 0)),
                pl.BlockSpec((1, rows, LANES), lambda f, pick, own: (f, 0, 0)),
                pl.BlockSpec((1, height, channels), lambda f, *_: (f, 0, 0)),
                pl.BlockSpec((1, height, channels), lambda f, *_: (f, 0, 0)),
                pl.BlockSpec((1, height, width, channels), lambda f, *_: (f, 0, 0, 0)),
                whole(w_edge.shape),
                whole(w_one.shape),
                whole(w_two.shape),
            ],
            out_specs=pl.BlockSpec((1, height, width, channels), lambda f, *_: (f, 0, 0, 0)),
            scratch_shapes=[
                pltpu.VMEM((-(-width // LANES), (height + 2) * SUB, LANES), jnp.float32),
                pltpu.VMEM((4, padded, channels), jnp.float32),
                pltpu.VMEM((height, 2 * channels), jnp.float32),
                pltpu.VMEM((3, height + 2, width, channels), jnp.bfloat16),
            ],
        ),
        compiler_params=pltpu.CompilerParams(vmem_limit_bytes=56 * 1024 * 1024),
        cost_estimate=pl.CostEstimate(
            flops=2 * frames * height * width * channels * (12 * channels + 64),
            bytes_accessed=4 * frames * height * width * channels,
            transcendentals=frames * height * width * channels,
        ),
    )(pick, own, near, far, left, right, activations, w_edge, w_one, w_two)


def dot(left, right, dims=((1,), (0,))):
    return lax.dot_general(left, right, (dims, ((), ())), preferred_element_type=WIDE)


def dot_rows(left, right):
    return dot(left, right, ((1,), (1,)))


def tower_kernel(
    tiles,
    pixel_ref,
    patch_ref,
    gain_ref,
    qkv_ref,
    proj_ref,
    post_gain_ref,
    text_ref,
    strip_ref,
    order_ref,
    patches_ref,
    unit_ref,
    scale_ref,
    normed_ref,
    heads_ref,
    head_scale_ref,
    probs_ref,
    column_ref,
    slope_ref,
    back_ref,
    grad_ref,
    tangent_ref,
):
    slots, colour_rows, columns = pixel_ref.shape
    height = colour_rows // 3
    dim = gain_ref.shape[1]
    across = columns // PATCH
    down = height // PATCH
    tokens = across * down
    bands = slots * down
    total = slots * tokens
    width = columns // tiles
    rem = max(width + 4 - LANES, 0)
    block = 2 * LANES

    column_id = lax.broadcasted_iota(jnp.int32, (columns, 1), 0)
    goal = (column_id % PATCH) * LANES + column_id // PATCH
    for j in range(PATCH):
        lane_id = lax.broadcasted_iota(jnp.int32, (columns, LANES), 1) + j * LANES
        order_ref[:, j * LANES : (j + 1) * LANES] = jnp.where(goal == lane_id, 1.0, 0.0).astype(
            NARROW
        )

    for f in range(slots):
        spread = dot(pixel_ref[f], order_ref[...])
        for py in range(down):
            entries = jnp.concatenate(
                [
                    spread[
                        k * height + py * PATCH : k * height + (py + 1) * PATCH,
                        j * LANES : (j + 1) * LANES,
                    ]
                    for j in range(PATCH)
                    for k in range(3)
                ],
                axis=0,
            )
            start = (f * down + py) * across
            patches_ref[start : start + across, :] = entries.T[:across].astype(NARROW)

    @pl.loop(0, dim // block)
    def _(n):
        at = pl.ds(pl.multiple_of(n * block, block), block)
        unit_ref[:, at] = dot(patches_ref[...], patch_ref[:, at])

    means = [jnp.zeros((1, dim), WIDE) for _ in range(slots)]
    for b in range(bands):
        rows = slice(b * across, (b + 1) * across)
        embedded = unit_ref[rows, :]
        means[b // down] += jnp.sum(embedded, axis=0, keepdims=True)
        centred = embedded - jnp.mean(embedded, axis=1, keepdims=True)
        scale = lax.rsqrt(jnp.mean(centred * centred, axis=1, keepdims=True) + EPS)
        unit = centred * scale
        unit_ref[rows, :] = unit
        scale_ref[rows, :] = jnp.broadcast_to(scale, (across, LANES))
        normed_ref[rows, :] = (unit * gain_ref[...]).astype(NARROW)
    means = [value * (1.0 / tokens) for value in means]

    row_head = lax.broadcasted_iota(jnp.int32, (LANES, LANES), 0) // HEAD_DIM
    lane_head = lax.broadcasted_iota(jnp.int32, (LANES, LANES), 1) // HEAD_DIM
    average = jnp.where(row_head == lane_head, 1.0 / HEAD_DIM, 0.0).astype(NARROW)

    @pl.loop(0, 2 * dim // block)
    def _(n):
        at = pl.multiple_of(n * block, block)
        both = dot(normed_ref[...], qkv_ref[:, pl.ds(at, block)])
        for i in range(2):
            part = both[:, i * LANES : (i + 1) * LANES]
            centred = part - dot(part.astype(NARROW), average)
            scale = lax.rsqrt(dot((centred * centred).astype(NARROW), average) + EPS)
            lanes = pl.ds(pl.multiple_of(at + i * LANES, LANES), LANES)
            head_scale_ref[:, lanes] = scale
            heads_ref[:, lanes] = (centred * scale).astype(NARROW)

    lane = lax.broadcasted_iota(jnp.int32, (1, LANES), 1)
    sides = [lane < HEAD_DIM, lane >= HEAD_DIM]
    factor = 1.0 / HEAD_DIM**0.5
    pairs = dim // LANES

    def pair_at(index):
        f = index // pairs
        i = index % pairs
        rows = pl.ds(pl.multiple_of(f * tokens, SUB), tokens)
        query_at = pl.ds(pl.multiple_of(i * LANES, LANES), LANES)
        key_at = pl.ds(pl.multiple_of(dim + i * LANES, LANES), LANES)
        return rows, query_at, key_at

    @pl.loop(0, slots * pairs)
    def _(index):
        rows, query_at, key_at = pair_at(index)
        query = heads_ref[rows, query_at]
        key = heads_ref[rows, key_at]
        for side in range(2):
            mask = jnp.where(sides[side], factor, 0.0).astype(NARROW)
            scores = dot_rows(query * mask, key)
            exps = jnp.exp(scores)
            probs = exps * (1.0 / jnp.sum(exps, axis=1, keepdims=True))
            column_ref[pl.ds(2 * index + side, 1), :] = jnp.sum(probs, axis=0, keepdims=True)
            probs_ref[2 * index + side] = probs.astype(NARROW)

    value_weight = qkv_ref.at[:, 2 * dim : 3 * dim]
    head_row = lax.broadcasted_iota(jnp.int32, (HEADS, dim), 0)
    head_lane = lax.broadcasted_iota(jnp.int32, (HEADS, dim), 1) // HEAD_DIM
    own_head = head_row == head_lane
    normed = [normed_ref[f * tokens : (f + 1) * tokens, :] for f in range(slots)]
    weights = [column_ref[f * HEADS : (f + 1) * HEADS, :].astype(NARROW) for f in range(slots)]
    mixed = jnp.concatenate([dot(weights[f], normed[f]) for f in range(slots)], axis=0)
    values = dot(mixed.astype(NARROW), value_weight[...])
    context = jnp.concatenate(
        [
            jnp.broadcast_to(
                jnp.sum(
                    jnp.where(own_head, values[f * HEADS : (f + 1) * HEADS], 0.0),
                    axis=0,
                    keepdims=True,
                )
                * (1.0 / tokens),
                (8, dim),
            )
            for f in range(slots)
        ],
        axis=0,
    )
    mean_rows = jnp.concatenate([jnp.broadcast_to(m, (8, dim)) for m in means], axis=0)
    pooled = mean_rows + dot(context.astype(NARROW), proj_ref[...])
    centred = pooled - jnp.mean(pooled, axis=1, keepdims=True)
    scale = lax.rsqrt(jnp.mean(centred * centred, axis=1, keepdims=True) + EPS)
    unit = centred * scale
    post = unit * post_gain_ref[...]
    text = text_ref[...]
    text = text * lax.rsqrt(jnp.sum(text * text, axis=1, keepdims=True) + EPS)
    along = jnp.sum(post * text, axis=1, keepdims=True)
    length = lax.rsqrt(jnp.sum(post * post, axis=1, keepdims=True) + EPS)
    post_back = (LOSS_SCALE * LOGIT_SCALE) * (length * text - along * length**3 * post)
    unit_back = post_back * post_gain_ref[...]
    pooled_back = scale * (
        unit_back
        - jnp.mean(unit_back, axis=1, keepdims=True)
        - unit * jnp.mean(unit_back * unit, axis=1, keepdims=True)
    )
    token_back = pooled_back * (1.0 / tokens)
    context_back = dot_rows(token_back.astype(NARROW), proj_ref[...])
    by_head = jnp.concatenate(
        [
            jnp.where(own_head, jnp.broadcast_to(context_back[8 * f : 8 * f + 1], (HEADS, dim)), 0.0)
            for f in range(slots)
        ],
        axis=0,
    )
    value_back = dot_rows(by_head.astype(NARROW), value_weight[...]).astype(NARROW)
    for f in range(slots):
        slope_ref[f * HEADS : (f + 1) * HEADS, :] = dot_rows(
            value_back[f * HEADS : (f + 1) * HEADS], normed[f]
        )

    def norm_back(gradient, rows, lanes):
        unit = heads_ref[rows, lanes].astype(WIDE)
        plain = dot(gradient.astype(NARROW), average)
        along = dot((gradient * unit).astype(NARROW), average)
        value = head_scale_ref[rows, lanes] * (gradient - plain - unit * along)
        back_ref[rows, lanes] = value.astype(NARROW)

    @pl.loop(0, slots * pairs)
    def _(index):
        rows, query_at, key_at = pair_at(index)
        query = heads_ref[rows, query_at]
        key = heads_ref[rows, key_at]
        query_back, key_back = [], []
        for side in range(2):
            probs = probs_ref[2 * index + side].astype(WIDE)
            slope = slope_ref[pl.ds(2 * index + side, 1), :]
            middle = jnp.sum(probs * slope, axis=1, keepdims=True)
            scores_back = (probs * (slope - middle) * factor).astype(NARROW)
            query_back.append(dot(scores_back, key))
            key_back.append(dot(scores_back, query, ((0,), (0,))))
        norm_back(jnp.where(sides[0], query_back[0], query_back[1]), rows, query_at)
        norm_back(jnp.where(sides[0], key_back[0], key_back[1]), rows, key_at)

    for f in range(slots):
        grad_ref[f * tokens : (f + 1) * tokens, :] = dot(
            weights[f], value_back[f * HEADS : (f + 1) * HEADS], ((0,), (0,))
        )

    @pl.loop(0, dim // block)
    def _(n):
        at = pl.ds(pl.multiple_of(n * block, block), block)
        grad_ref[:, at] += dot_rows(back_ref[...], qkv_ref[at, : 2 * dim])

    tangent_ref[...] = jnp.zeros_like(tangent_ref)
    for b in range(bands):
        rows = slice(b * across, (b + 1) * across)
        f = b // down
        unit = unit_ref[rows, :]
        unit_back = grad_ref[rows, :] * gain_ref[...]
        value = (
            unit_back
            - jnp.mean(unit_back, axis=1, keepdims=True)
            - unit * jnp.mean(unit_back * unit, axis=1, keepdims=True)
        )
        value = scale_ref[rows, :1] * value + token_back[8 * f : 8 * f + 1]
        tangent_ref[b * LANES : b * LANES + across, :] = value.astype(NARROW)

    for f in range(slots):
        entries = dot_rows(
            patch_ref[...], tangent_ref[f * down * LANES : (f + 1) * down * LANES, :]
        ).astype(NARROW)
        lines = []
        for k in range(3):
            for py in range(down):
                lines.append(
                    jnp.concatenate(
                        [
                            entries[
                                (3 * j + k) * PATCH : (3 * j + k + 1) * PATCH,
                                py * LANES : (py + 1) * LANES,
                            ]
                            for j in range(PATCH)
                        ],
                        axis=1,
                    )
                )
        frame = dot_rows(jnp.concatenate(lines, axis=0), order_ref[...])
        frame = jnp.concatenate(
            [
                jnp.zeros((colour_rows, 2), WIDE),
                frame,
                jnp.zeros((colour_rows, LANES - 2), WIDE),
            ],
            axis=1,
        )
        for t in range(tiles):
            base = t * width
            main = frame[:, base : base + LANES]
            if rem == 0 and width + 4 < LANES:
                main = jnp.where(lane < width + 4, main, 0.0)
            strip_ref[t, f, :colour_rows, :] = main.astype(NARROW)
            if rem > 0:
                tail = [
                    frame[
                        k * height : (k + 1) * height, base + LANES : base + LANES + rem
                    ]
                    for k in range(3)
                ]
                tail.append(jnp.zeros((height, LANES - 3 * rem), WIDE))
                strip_ref[t, f, colour_rows:, :] = jnp.concatenate(tail, axis=1).astype(NARROW)


def tower(
    pixels, patch_weight, norm_gain, qkv_weight, out_weight, post_gain, text_embed, tiles
):
    slots, colours, height, columns = pixels.shape
    dim = norm_gain.shape[0]
    across = columns // PATCH
    down = height // PATCH
    tokens = across * down
    total = slots * tokens
    width = columns // tiles
    rows = colours * height + (height if width + 4 > LANES else 0)
    entries = colours * PATCH * PATCH
    reordered = (
        patch_weight.reshape(colours * PATCH, PATCH, dim).transpose(1, 0, 2).reshape(entries, dim)
    )
    vmem = pl.BlockSpec(memory_space=pltpu.VMEM)
    return pl.pallas_call(
        functools.partial(tower_kernel, tiles),
        out_shape=jax.ShapeDtypeStruct((tiles, slots, rows, LANES), NARROW),
        in_specs=[vmem] * 7,
        out_specs=vmem,
        scratch_shapes=[
            pltpu.VMEM((columns, PATCH * LANES), NARROW),
            pltpu.VMEM((total, entries), NARROW),
            pltpu.VMEM((total, dim), WIDE),
            pltpu.VMEM((total, LANES), WIDE),
            pltpu.VMEM((total, dim), NARROW),
            pltpu.VMEM((total, 2 * dim), NARROW),
            pltpu.VMEM((total, 2 * dim), WIDE),
            pltpu.VMEM((slots * HEADS, tokens, tokens), NARROW),
            pltpu.VMEM((slots * HEADS, tokens), WIDE),
            pltpu.VMEM((slots * HEADS, tokens), WIDE),
            pltpu.VMEM((total, 2 * dim), NARROW),
            pltpu.VMEM((total, dim), WIDE),
            pltpu.VMEM((slots * down * LANES, dim), NARROW),
        ],
        compiler_params=pltpu.CompilerParams(vmem_limit_bytes=60 * 1024 * 1024),
        cost_estimate=pl.CostEstimate(
            flops=2 * total * dim * (2 * entries + 4 * dim + 4 * tokens),
            bytes_accessed=2 * (entries * dim + 4 * dim * dim),
            transcendentals=slots * HEADS * tokens * tokens,
        ),
    )(
        pixels.reshape(slots, colours * height, columns),
        reordered,
        norm_gain[None],
        qkv_weight,
        out_weight,
        post_gain[None],
        text_embed[None],
    )


def frame_rank(owner):
    frame_ids = jnp.arange(owner.shape[0], dtype=jnp.int32)
    same_owner = owner[:, None] == owner[None, :]
    earlier = frame_ids[None, :] < frame_ids[:, None]
    return jnp.sum((same_owner & earlier).astype(jnp.int32), axis=1)


def local(
    pixels,
    owner,
    patch_weight,
    norm_gain,
    qkv_weight,
    out_weight,
    post_gain,
    text_embed,
    conv_out_weight,
    conv_weight,
    activations,
):
    tile_count = lax.axis_size("tile")
    core_count = lax.axis_size("tm")
    core = lax.axis_index("tm")
    tile = lax.axis_index("tile")
    frames, height, width, channels = activations.shape
    slots = pixels.shape[0]
    ranks_all = frame_rank(owner)

    up = [(i, i + 1) for i in range(tile_count - 1)]
    down = [(j, i) for i, j in up]
    outside = jnp.asarray(-30000.0, activations.dtype)
    left = lax.ppermute(activations[:, :, width - 1], "tile", up)
    right = lax.ppermute(activations[:, :, 0], "tile", down)
    left = jnp.where(tile == 0, outside, left)
    right = jnp.where(tile == tile_count - 1, outside, right)

    outgoing = tower(
        pixels, patch_weight, norm_gain, qkv_weight, out_weight, post_gain, text_embed, tile_count
    )
    rows = outgoing.shape[2]
    near = lax.all_to_all(outgoing, "tile", split_axis=0, concat_axis=0, tiled=True)
    near = near.reshape(tile_count * slots, rows, LANES)
    pick_all = (owner // core_count) * slots + ranks_all
    own_all = owner % core_count
    by_core = lambda values, index: lax.dynamic_slice_in_dim(values, index * frames, frames)
    other = 1 - core
    far = lax.ppermute(jnp.take(near, by_core(pick_all, other), axis=0), "tm", [(0, 1), (1, 0)])
    return decode(
        by_core(pick_all, core),
        (by_core(own_all, core) == core).astype(jnp.int32),
        near,
        far,
        left,
        right,
        activations,
        conv_out_weight,
        conv_weight,
        4,
    )


def solution(mesh):
    placed = (
        P(("groups", "tile", "tm"), None, None, None),
        P("groups"),
        P(),
        P(),
        P(),
        P(),
        P(),
        P("groups"),
        P(),
        P(),
        P(("groups", "tm"), None, "tile", None),
    )
    return jax.shard_map(
        local,
        mesh=mesh,
        in_specs=placed,
        out_specs=P(("groups", "tm"), None, "tile", None),
        check_vma=False,
    )
```

profile of v0, /device:TPU:1, one launch (start us, length us, event | category | flops | bytes accessed | tf_op | source)
XLA Modules:
  0.0 151.5 jit_solution(736948583831219768)
XLA Ops:
  0.0 0.0 copy-start.1
  0.0 2.2 %fusion.1 = (bf16[8,64,1,128]{3,2,1,0:T(2,128)(2,1)S(1)}, bf16[8,64,1,128]{3,2,1,0:T(2,128)(2,1)S(1)}) fusion(bf16[8,64,160,128]{3,2,1,0:T(8,128)(2,1)} %act_ref.1), kind=kLoop, calls=%fused_computation.67 | loop fusion | bytes 524288 | tf_op jit(solution)/shard_map/slice | solution.py:589
  2.2 4.0 %collective-permute-start.1 = (bf16[8,64,128]{2,1,0:T(8,128)(2,1)S(1)}, bf16[8,64,128]{2,1,0:T(8,128)(2,1)S(1)}, u32[]{:S(2)}, u32[]{:S(2)}) collective-permute-start(bf16[8,64,128]{2,1,0:T(8,128)(2,1)S(1)} %bitcast.102), channel_id=1, source_target_pairs={{0,2},{2,4},{4,6},{6,8},{8,10},{10,12},{12,14},{1,3},{3,5},{5,7},{... | collective-permute-start | bytes 393224 | tf_op jit(solution)/shard_map/ppermute | solution.py:588
  6.2 1.3 collective-permute-start.2
  7.5 0.0 copy-done.1
  7.5 2.0 %copy.24 = bf16[48,16,1024]{2,0,1:T(8,128)(2,1)} copy(bf16[48,16,1024]{2,1,0:T(8,128)(2,1)S(1)} %bitcast.98) | data formatting | bytes 3145728 | tf_op jit(solution)/shard_map/reshape | solution.py:517
  9.6 51.9 %shard_map.109 = bf16[8,2,256,128]{3,2,1,0:T(8,128)(2,1)} custom-call(bf16[2,192,1280]{2,1,0:T(8,128)(2,1)} %bitcast.111, bf16[768,1024]{1,0:T(8,128)(2,1)} %bitcast.99, f32[1,1024]{1,0:T(1,128)} %bitcast.112, bf16[1024,3072]{1,0:T(8,128)(2,1)} %qkv_ref.1, bf16[1024,1024]{1,0:T(8,128)(2,1)} %proj_ref.1, f32[1,1024]{1,0:T(1,128)} %bitcast.113, ...), custom_call_target="tpu_custom_call" | custom-call | flops 9059696640 | bytes 9961472 | tf_op jit(solution)/shard_map/pallas_call | solution.py:520
  61.4 0.0 copy-start.3
  61.4 0.0 copy-start.2
  61.4 6.5 %all-to-all-start = ((bf16[8,2,256,128]{3,2,1,0:T(8,128)(2,1)}), bf16[8,2,256,128]{3,2,1,0:T(8,128)(2,1)S(1)}, u32[]{:S(2)}, u32[]{:S(2)}) async-start(bf16[8,2,256,128]{3,2,1,0:T(8,128)(2,1)} %shard_map.109), calls=%async_computation | async-start | bytes 2097152 | tf_op jit(solution)/shard_map/all_to_all | solution.py:597
  68.0 0.0 copy-done.3
  68.1 0.1 maximum_maximum_fusion.1
  68.2 0.6 copy.29
  69.0 0.0 copy-done.2
  69.0 0.0 copy-start.5
  69.1 0.2 maximum_maximum_fusion
  69.3 1.2 copy.30
  70.5 0.0 copy-done.5
  70.5 0.2 convert_reduce_fusion
  70.7 0.7 dynamic_slice.9.pick_ref
  71.8 0.3 scatter.161
  72.1 0.1 scatter.141
  72.2 0.1 scatter.164
  72.3 0.1 scatter.144
  72.5 0.1 scatter.121
  72.6 0.1 scatter.124
  72.9 0.1 compare_and_fusion
  73.3 0.0 copy-start.4
  73.3 19.2 %all-to-all-done = bf16[8,2,256,128]{3,2,1,0:T(8,128)(2,1)S(1)} async-done(((bf16[8,2,256,128]{3,2,1,0:T(8,128)(2,1)}), bf16[8,2,256,128]{3,2,1,0:T(8,128)(2,1)S(1)}, u32[]{:S(2)}, u32[]{:S(2)}) %all-to-all-start) | async-done | bytes 1048608 | tf_op jit(solution)/shard_map/all_to_all | solution.py:597
  92.4 0.0 copy-done.4
  92.4 0.0 copy-start
  92.4 0.6 gather_fusion
  93.1 0.1 broadcast_select_fusion
  93.2 2.5 %collective-permute-start = (bf16[8,256,128]{2,1,0:T(8,128)(2,1)S(1)}, bf16[8,256,128]{2,1,0:T(8,128)(2,1)S(1)}, u32[]{:S(2)}, u32[]{:S(2)}) collective-permute-start(bf16[8,256,128]{2,1,0:T(8,128)(2,1)S(1)} %broadcast_select_fusion), channel_id=1, source_target_pairs={{0,1},{1,0},{2,3},{3,2},{4,5},{5,4},{6,7},{7,6},{8,9},{9,8},{10,11... | collective-permute-start | bytes 1572872 | tf_op jit(solution)/shard_map/ppermute | solution.py:603
  95.7 0.7 compare_convert_fusion.own_ref
  96.4 0.0 collective-permute-done.1
  96.4 0.7 broadcast_select_fusion.2.left_ref
  97.1 0.0 collective-permute-done.2
  97.1 0.7 broadcast_select_fusion.1.right_ref
  97.7 0.0 collective-permute-done.far_ref
  97.7 0.0 copy-start.6
  97.7 0.0 copy-done
  97.8 0.8 copy-done.6
  98.6 52.9 %shard_map.110 = bf16[8,64,160,128]{3,2,1,0:T(8,128)(2,1)} custom-call(s32[8]{0:T(128)} %dynamic_slice.9.pick_ref, s32[8]{0:T(128)} %compare_convert_fusion.own_ref, bf16[16,256,128]{2,1,0:T(8,128)(2,1)} %bitcast.97, bf16[8,256,128]{2,1,0:T(8,128)(2,1)} %copy-done.6, bf16[8,64,128]{2,1,0:T(8,128)(2,1)} %broadcast_select_fusion.2.left_ref, ...), custom_call_target="tpu_custom_call" | custom-call | flops 33554432000 | bytes 41943040 | tf_op jit(solution)/shard_map/pallas_call | solution.py:195
  (50 shorter events, 1.2 us)
Async XLA Ops:
  0.0 7.5 %copy-start.1 = (bf16[768,1024]{1,0:T(8,128)(2,1)S(1)}, bf16[768,1024]{1,0:T(8,128)(2,1)}, u32[]{:S(2)}) copy-start(bf16[768,1024]{1,0:T(8,128)(2,1)} %param.85) | copy-start | bytes 4718596
  2.2 94.2 %collective-permute-start.1 = (bf16[8,64,128]{2,1,0:T(8,128)(2,1)S(1)}, bf16[8,64,128]{2,1,0:T(8,128)(2,1)S(1)}, u32[]{:S(2)}, u32[]{:S(2)}) collective-permute-start(bf16[8,64,128]{2,1,0:T(8,128)(2,1)S(1)} %bitcast.102), channel_id=1, source_target_pairs={{0,2},{2,4},{4,6},{6,8},{8,10},{10,12},{12,14},{1,3},{3,5},{5,7},{... | collective-permute-start | bytes 393224 | tf_op jit(solution)/shard_map/ppermute | solution.py:588
  6.2 90.9 %collective-permute-start.2 = (bf16[8,64,128]{2,1,0:T(8,128)(2,1)S(1)}, bf16[8,64,128]{2,1,0:T(8,128)(2,1)S(1)}, u32[]{:S(2)}, u32[]{:S(2)}) collective-permute-start(bf16[8,64,128]{2,1,0:T(8,128)(2,1)S(1)} %bitcast.103), channel_id=1, source_target_pairs={{2,0},{4,2},{6,4},{8,6},{10,8},{12,10},{14,12},{3,1},{5,3},{7,5},{... | collective-permute-start | bytes 393224 | tf_op jit(solution)/shard_map/ppermute | solution.py:589
  61.4 6.5 %copy-start.3 = (bf16[3,3,128,3]{2,3,1,0:T(4,128)(2,1)S(1)}, bf16[3,3,128,3]{2,3,1,0:T(4,128)(2,1)}, u32[]{:S(2)}) copy-start(bf16[3,3,128,3]{2,3,1,0:T(4,128)(2,1)} %param.91) | copy-start | bytes 20740
  61.4 7.6 %copy-start.2 = (bf16[3,3,128,128]{3,2,1,0:T(8,128)(2,1)S(1)}, bf16[3,3,128,128]{3,2,1,0:T(8,128)(2,1)}, u32[]{:S(2)}) copy-start(bf16[3,3,128,128]{3,2,1,0:T(8,128)(2,1)} %param.92) | copy-start | bytes 884740
  61.4 31.0 %all-to-all-start = ((bf16[8,2,256,128]{3,2,1,0:T(8,128)(2,1)}), bf16[8,2,256,128]{3,2,1,0:T(8,128)(2,1)S(1)}, u32[]{:S(2)}, u32[]{:S(2)}) async-start(bf16[8,2,256,128]{3,2,1,0:T(8,128)(2,1)} %shard_map.109), calls=%async_computation | async-start | bytes 2097152 | tf_op jit(solution)/shard_map/all_to_all | solution.py:597
  69.0 1.4 copy-start.5
  73.3 19.2 %copy-start.4 = (bf16[512,768]{1,0:T(8,128)(2,1)}, bf16[512,768]{1,0:T(8,128)(2,1)S(1)}, u32[]{:S(2)}) copy-start(bf16[512,768]{1,0:T(8,128)(2,1)S(1)} %constant_dynamic-update-slice_fusion.w_edge_ref) | copy-start | bytes 2359300
  92.4 5.3 %copy-start = (bf16[8,2,256,128]{3,2,1,0:T(8,128)(2,1)}, bf16[8,2,256,128]{3,2,1,0:T(8,128)(2,1)S(1)}, u32[]{:S(2)}) copy-start(bf16[8,2,256,128]{3,2,1,0:T(8,128)(2,1)S(1)} %all-to-all-done) | copy-start | bytes 3145732
  93.2 4.5 %collective-permute-start = (bf16[8,256,128]{2,1,0:T(8,128)(2,1)S(1)}, bf16[8,256,128]{2,1,0:T(8,128)(2,1)S(1)}, u32[]{:S(2)}, u32[]{:S(2)}) collective-permute-start(bf16[8,256,128]{2,1,0:T(8,128)(2,1)S(1)} %broadcast_select_fusion), channel_id=1, source_target_pairs={{0,1},{1,0},{2,3},{3,2},{4,5},{5,4},{6,7},{7,6},{8,9},{9,8},{10,11... | collective-permute-start | bytes 1572872 | tf_op jit(solution)/shard_map/ppermute | solution.py:603
  97.7 0.8 copy-start.6
where the time goes:
time: 152 us; the launch traced here: 151 us
  Pallas kernels  105 us (69%)
  waiting for transfers between devices  19.2 us (13%)
  starting transfers between devices  14.3 us (9%)
  local copies, waits for them, and re-layouts  10.2 us (7%)
  other arithmetic  2.65 us (2%)
    pallas_call x1, Pallas kernels, decode(): pl.pallas_call(functools.partial(decoder_kernel, height, width, block_row...  52.9 us
    pallas_call x1, Pallas kernels, tower(): pl.pallas_call(functools.partial(tower_kernel, tiles), out_shape=jax.Shap...  51.9 us
    all_to_all x1, waiting for transfers between devices, local(): lax.all_to_all(outgoing, 'tile', split_axis=0, concat_axis=0, tiled=True)  19.2 us
    all_to_all x1, starting transfers between devices, local(): lax.all_to_all(outgoing, 'tile', split_axis=0, concat_axis=0, tiled=True)  6.53 us
    ppermute x1, starting transfers between devices, local(): left = lax.ppermute(activations[:, :, width - 1], 'tile', up)  3.98 us
  transfers between devices with their start and end apart: 4, of which 1 were waited for; matrix products, arithmetic and copies ran while one was open for 6% of the time, Pallas kernels for 34%

commit v1 on v0

--- a/solution.py
+++ b/solution.py
@@ -21,8 +21,9 @@
 
 
 def silu_slope(pre_value):
-    half = jnp.tanh(0.5 * pre_value)
-    return 0.5 + 0.5 * half + (0.25 * pre_value) * (1.0 - half * half)
+    half = 0.5 * pre_value
+    gate = jnp.tanh(half)
+    return (1.0 + gate) * (1.0 + half * (1.0 - gate))
 
 
 def decoder_kernel(
@@ -144,7 +145,7 @@
 
 def decoder_weights(conv_out_weight, conv_weight, height, width):
     rem = max(width + 4 - LANES, 0)
-    taps_out = conv_out_weight.transpose(0, 1, 3, 2)
+    taps_out = 0.5 * conv_out_weight.transpose(0, 1, 3, 2)
     channels = conv_weight.shape[2]
     small = jnp.pad(
         taps_out.reshape(3, 9, channels), ((0, 0), (0, SUB - 9), (0, 0))
@@ -236,7 +237,7 @@
 def tower_kernel(
     tiles,
     pixel_ref,
-    patch_ref,
+    patch_raw_ref,
     gain_ref,
     qkv_ref,
     proj_ref,
@@ -256,7 +257,15 @@
     back_ref,
     grad_ref,
     tangent_ref,
+    qkv_copy_ref,
+    proj_copy_ref,
+    patch_order_ref,
+    sems,
 ):
+    qkv_copy = pltpu.make_async_copy(qkv_ref, qkv_copy_ref, sems.at[0])
+    proj_copy = pltpu.make_async_copy(proj_ref, proj_copy_ref, sems.at[1])
+    qkv_copy.start()
+    proj_copy.start()
     slots, colour_rows, columns = pixel_ref.shape
     height = colour_rows // 3
     dim = gain_ref.shape[1]
@@ -276,6 +285,17 @@
         order_ref[:, j * LANES : (j + 1) * LANES] = jnp.where(goal == lane_id, 1.0, 0.0).astype(
             NARROW
         )
+
+    entries_count = patch_raw_ref.shape[0]
+    row_id = lax.broadcasted_iota(jnp.int32, (entries_count, 1), 0)
+    lines_count = entries_count // PATCH
+    goal = (row_id % lines_count) * PATCH + row_id // lines_count
+    entry_id = lax.broadcasted_iota(jnp.int32, (entries_count, entries_count), 1)
+    move = jnp.where(goal == entry_id, 1.0, 0.0).astype(NARROW)
+    patch_ref = patch_order_ref
+    for n in range(dim // block):
+        at = slice(n * block, (n + 1) * block)
+        patch_ref[:, at] = dot(move, patch_raw_ref[:, at]).astype(NARROW)
 
     for f in range(slots):
         spread = dot(pixel_ref[f], order_ref[...])
@@ -294,7 +314,7 @@
             start = (f * down + py) * across
             patches_ref[start : start + across, :] = entries.T[:across].astype(NARROW)
 
-    @pl.loop(0, dim // block)
+    @pl.loop(0, dim // block, unroll=2)
     def _(n):
         at = pl.ds(pl.multiple_of(n * block, block), block)
         unit_ref[:, at] = dot(patches_ref[...], patch_ref[:, at])
@@ -312,21 +332,22 @@
         normed_ref[rows, :] = (unit * gain_ref[...]).astype(NARROW)
     means = [value * (1.0 / tokens) for value in means]
 
-    row_head = lax.broadcasted_iota(jnp.int32, (LANES, LANES), 0) // HEAD_DIM
-    lane_head = lax.broadcasted_iota(jnp.int32, (LANES, LANES), 1) // HEAD_DIM
+    qkv_copy.wait()
+    proj_copy.wait()
+    qkv_ref, proj_ref = qkv_copy_ref, proj_copy_ref
+
+    row_head = lax.broadcasted_iota(jnp.int32, (block, block), 0) // HEAD_DIM
+    lane_head = lax.broadcasted_iota(jnp.int32, (block, block), 1) // HEAD_DIM
     average = jnp.where(row_head == lane_head, 1.0 / HEAD_DIM, 0.0).astype(NARROW)
 
     @pl.loop(0, 2 * dim // block)
     def _(n):
         at = pl.multiple_of(n * block, block)
         both = dot(normed_ref[...], qkv_ref[:, pl.ds(at, block)])
-        for i in range(2):
-            part = both[:, i * LANES : (i + 1) * LANES]
-            centred = part - dot(part.astype(NARROW), average)
-            scale = lax.rsqrt(dot((centred * centred).astype(NARROW), average) + EPS)
-            lanes = pl.ds(pl.multiple_of(at + i * LANES, LANES), LANES)
-            head_scale_ref[:, lanes] = scale
-            heads_ref[:, lanes] = (centred * scale).astype(NARROW)
+        centred = both - dot(both.astype(NARROW), average)
+        scale = lax.rsqrt(dot((centred * centred).astype(NARROW), average) + EPS)
+        head_scale_ref[:, pl.ds(at, block)] = scale
+        heads_ref[:, pl.ds(at, block)] = (centred * scale).astype(NARROW)
 
     lane = lax.broadcasted_iota(jnp.int32, (1, LANES), 1)
     sides = [lane < HEAD_DIM, lane >= HEAD_DIM]
@@ -341,7 +362,7 @@
         key_at = pl.ds(pl.multiple_of(dim + i * LANES, LANES), LANES)
         return rows, query_at, key_at
 
-    @pl.loop(0, slots * pairs)
+    @pl.loop(0, slots * pairs, unroll=16)
     def _(index):
         rows, query_at, key_at = pair_at(index)
         query = heads_ref[rows, query_at]
@@ -409,14 +430,7 @@
             value_back[f * HEADS : (f + 1) * HEADS], normed[f]
         )
 
-    def norm_back(gradient, rows, lanes):
-        unit = heads_ref[rows, lanes].astype(WIDE)
-        plain = dot(gradient.astype(NARROW), average)
-        along = dot((gradient * unit).astype(NARROW), average)
-        value = head_scale_ref[rows, lanes] * (gradient - plain - unit * along)
-        back_ref[rows, lanes] = value.astype(NARROW)
-
-    @pl.loop(0, slots * pairs)
+    @pl.loop(0, slots * pairs, unroll=16)
     def _(index):
         rows, query_at, key_at = pair_at(index)
         query = heads_ref[rows, query_at]
@@ -426,18 +440,29 @@
             probs = probs_ref[2 * index + side].astype(WIDE)
             slope = slope_ref[pl.ds(2 * index + side, 1), :]
             middle = jnp.sum(probs * slope, axis=1, keepdims=True)
-            scores_back = (probs * (slope - middle) * factor).astype(NARROW)
+            scores_back = (probs * (slope - middle)).astype(NARROW)
             query_back.append(dot(scores_back, key))
             key_back.append(dot(scores_back, query, ((0,), (0,))))
-        norm_back(jnp.where(sides[0], query_back[0], query_back[1]), rows, query_at)
-        norm_back(jnp.where(sides[0], key_back[0], key_back[1]), rows, key_at)
+        gradient = jnp.concatenate(
+            [
+                jnp.where(sides[0], query_back[0], query_back[1]),
+                jnp.where(sides[0], key_back[0], key_back[1]),
+            ],
+            axis=1,
+        )
+        unit = jnp.concatenate([query, key], axis=1).astype(WIDE)
+        plain = dot(gradient.astype(NARROW), average)
+        along = dot((gradient * unit).astype(NARROW), average)
+        value = factor * (gradient - plain - unit * along)
+        back_ref[rows, query_at] = (head_scale_ref[rows, query_at] * value[:, :LANES]).astype(NARROW)
+        back_ref[rows, key_at] = (head_scale_ref[rows, key_at] * value[:, LANES:]).astype(NARROW)
 
     for f in range(slots):
         grad_ref[f * tokens : (f + 1) * tokens, :] = dot(
             weights[f], value_back[f * HEADS : (f + 1) * HEADS], ((0,), (0,))
         )
 
-    @pl.loop(0, dim // block)
+    @pl.loop(0, dim // block, unroll=2)
     def _(n):
         at = pl.ds(pl.multiple_of(n * block, block), block)
         grad_ref[:, at] += dot_rows(back_ref[...], qkv_ref[at, : 2 * dim])
@@ -513,14 +538,11 @@
     width = columns // tiles
     rows = colours * height + (height if width + 4 > LANES else 0)
     entries = colours * PATCH * PATCH
-    reordered = (
-        patch_weight.reshape(colours * PATCH, PATCH, dim).transpose(1, 0, 2).reshape(entries, dim)
-    )
     vmem = pl.BlockSpec(memory_space=pltpu.VMEM)
     return pl.pallas_call(
         functools.partial(tower_kernel, tiles),
         out_shape=jax.ShapeDtypeStruct((tiles, slots, rows, LANES), NARROW),
-        in_specs=[vmem] * 7,
+        in_specs=[vmem] * 3 + [pl.BlockSpec(memory_space=pl.ANY)] * 2 + [vmem] * 2,
         out_specs=vmem,
         scratch_shapes=[
             pltpu.VMEM((columns, PATCH * LANES), NARROW),
@@ -536,6 +558,10 @@
             pltpu.VMEM((total, 2 * dim), NARROW),
             pltpu.VMEM((total, dim), WIDE),
             pltpu.VMEM((slots * down * LANES, dim), NARROW),
+            pltpu.VMEM(qkv_weight.shape, NARROW),
+            pltpu.VMEM(out_weight.shape, NARROW),
+            pltpu.VMEM((entries, dim), NARROW),
+            pltpu.SemaphoreType.DMA((2,)),
         ],
         compiler_params=pltpu.CompilerParams(vmem_limit_bytes=60 * 1024 * 1024),
         cost_estimate=pl.CostEstimate(
@@ -545,7 +571,7 @@
         ),
     )(
         pixels.reshape(slots, colours * height, columns),
-        reordered,
+        patch_weight,
         norm_gain[None],
         qkv_weight,
         out_weight,
@@ -582,19 +608,20 @@
     slots = pixels.shape[0]
     ranks_all = frame_rank(owner)
 
+    outgoing = tower(
+        pixels, patch_weight, norm_gain, qkv_weight, out_weight, post_gain, text_embed, tile_count
+    )
+    outgoing, origin = lax.optimization_barrier((outgoing, jnp.int32(0)))
+    rows = outgoing.shape[2]
+    near = lax.all_to_all(outgoing, "tile", split_axis=0, concat_axis=0, tiled=True)
     up = [(i, i + 1) for i in range(tile_count - 1)]
     down = [(j, i) for i, j in up]
     outside = jnp.asarray(-30000.0, activations.dtype)
-    left = lax.ppermute(activations[:, :, width - 1], "tile", up)
-    right = lax.ppermute(activations[:, :, 0], "tile", down)
+    left = lax.ppermute(lax.dynamic_index_in_dim(activations, origin + (width - 1), 2, False), "tile", up)
+    right = lax.ppermute(lax.dynamic_index_in_dim(activations, origin, 2, False), "tile", down)
     left = jnp.where(tile == 0, outside, left)
     right = jnp.where(tile == tile_count - 1, outside, right)
 
-    outgoing = tower(
-        pixels, patch_weight, norm_gain, qkv_weight, out_weight, post_gain, text_embed, tile_count
-    )
-    rows = outgoing.shape[2]
-    near = lax.all_to_all(outgoing, "tile", split_axis=0, concat_axis=0, tiled=True)
     near = near.reshape(tile_count * slots, rows, LANES)
     pick_all = (owner // core_count) * slots + ranks_all
     own_all = owner % core_count

time: 152 us -> 132 us (0.87)
  Pallas kernels: 105 us -> 93.2 us
  waiting for transfers between devices: 19.2 us -> 8.81 us
  local copies, waits for them, and re-layouts: 10.2 us -> 11.8 us
    all_to_all x1, waiting for transfers between devices: 19.2 us -> 8.8 us  [local(): lax.all_to_all(outgoing, 'tile', split_axis=0, concat_axis=0, tiled=True)]
    pallas_call x1, Pallas kernels: 51.9 us -> 42.7 us  [tower(): pl.pallas_call(functools.partial(tower_kernel, tiles), out_shape=jax.Shap...]
    unnamed x22 -> x18, local copies, waits for them, and re-layouts: 1.03 us -> 4.32 us
    pallas_call x1, Pallas kernels: 52.9 us -> 50.5 us  [decode(): pl.pallas_call(functools.partial(decoder_kernel, height, width, block_row...]
    slice x1 -> x0, local copies, waits for them, and re-layouts: 2.18 us -> none  [local(): right = lax.ppermute(activations[:, :, 0], 'tile', down)]
    dynamic_slice x0 -> x1, local copies, waits for them, and re-layouts: none -> 2.02 us  [local(): lax.dynamic_index_in_dim(activations, origin, 2, False)]
    reshape x1 -> x0, local copies, waits for them, and re-layouts: 2.01 us -> none  [tower(): patch_weight.reshape(colours * PATCH, PATCH, dim).transpose(1, 0, 2)]
  transfers between devices with their start and end apart: 4 -> 4, of which waited for: 1 -> 1; matrix products, arithmetic and copies ran while one was open for 6% -> 10% of each run, Pallas kernels for 34% -> 0%
where the time goes in v1:
time: 132 us; the launch traced here: 131 us
  Pallas kernels  93.2 us (71%)
  starting transfers between devices  14.6 us (11%)
  local copies, waits for them, and re-layouts  11.8 us (9%)
  waiting for transfers between devices  8.81 us (7%)
  other arithmetic  2.6 us (2%)
    pallas_call x1, Pallas kernels, decode(): pl.pallas_call(functools.partial(decoder_kernel, height, width, block_row...  50.5 us
    pallas_call x1, Pallas kernels, tower(): pl.pallas_call(functools.partial(tower_kernel, tiles), out_shape=jax.Shap...  42.7 us
    all_to_all x1, waiting for transfers between devices, local(): lax.all_to_all(outgoing, 'tile', split_axis=0, concat_axis=0, tiled=True)  8.8 us
    all_to_all x1, starting transfers between devices, local(): lax.all_to_all(outgoing, 'tile', split_axis=0, concat_axis=0, tiled=True)  6.39 us
    unnamed x18, local copies, waits for them, and re-layouts  4.32 us
    ppermute x1, starting transfers between devices, local(): lax.ppermute(jnp.take(near, by_core(pick_all, other), axis=0), 'tm', [(0,...  3.59 us
    ppermute x1, starting transfers between devices, local(): lax.ppermute(lax.dynamic_index_in_dim(activations, origin + (width - 1),...  3.37 us
  transfers between devices with their start and end apart: 4, of which 1 were waited for; matrix products, arithmetic and copies ran while one was open for 10% of the time, Pallas kernels for 0%

profile of v1, /device:TPU:1, one launch (start us, length us, event | category | flops | bytes accessed | tf_op | source)
XLA Modules:
  0.0 131.3 jit_solution(9601984764459137167)
XLA Ops:
  0.0 42.7 %shard_map.109 = bf16[8,2,256,128]{3,2,1,0:T(8,128)(2,1)} custom-call(bf16[2,192,1280]{2,1,0:T(8,128)(2,1)} %bitcast.103, bf16[768,1024]{1,0:T(8,128)(2,1)} %patch_raw_ref.1, f32[1,1024]{1,0:T(1,128)} %bitcast.104, bf16[1024,3072]{1,0:T(8,128)(2,1)} %qkv_ref.1, bf16[1024,1024]{1,0:T(8,128)(2,1)} %proj_ref.1, f32[1,1024]{1,0:T(1,128)} %bitcast.105, ...), custom_call_target="tpu_custom_call" | custom-call | flops 9059696640 | bytes 9961472 | tf_op jit(solution)/shard_map/pallas_call | solution.py:542
  42.7 0.0 copy-start.2
  42.7 6.4 %all-to-all-start = ((bf16[8,2,256,128]{3,2,1,0:T(8,128)(2,1)}), bf16[8,2,256,128]{3,2,1,0:T(8,128)(2,1)S(1)}, u32[]{:S(2)}, u32[]{:S(2)}) async-start(bf16[8,2,256,128]{3,2,1,0:T(8,128)(2,1)} %shard_map.109), calls=%async_computation | async-start | bytes 2097152 | tf_op jit(solution)/shard_map/all_to_all | solution.py:616
  49.1 0.0 copy-start.1
  49.1 2.0 %constant_dynamic-slice_fusion = (bf16[8,64,1,128]{3,2,1,0:T(2,128)(2,1)S(1)}, bf16[8,64,1,128]{3,2,1,0:T(2,128)(2,1)S(1)}) fusion(bf16[8,64,160,128]{3,2,1,0:T(8,128)(2,1)} %act_ref.1, s32[]{:T(128)S(6)} %select_n.59, s32[]{:T(128)S(6)} %select_n.56), kind=kLoop, calls=%fused_computation.69 | loop fusion | bytes 524296 | tf_op jit(solution)/shard_map/jit(dynamic_index_in_dim)/dynamic_slice | solution.py:621
  51.2 3.4 %collective-permute-start.1 = (bf16[8,64,128]{2,1,0:T(8,128)(2,1)S(1)}, bf16[8,64,128]{2,1,0:T(8,128)(2,1)S(1)}, u32[]{:S(2)}, u32[]{:S(2)}) collective-permute-start(bf16[8,64,128]{2,1,0:T(8,128)(2,1)S(1)} %bitcast.98), channel_id=1, source_target_pairs={{0,2},{2,4},{4,6},{6,8},{8,10},{10,12},{12,14},{1,3},{3,5},{5,7},{... | collective-permute-start | bytes 393224 | tf_op jit(solution)/shard_map/ppermute | solution.py:620
  54.6 1.3 collective-permute-start.2
  55.9 0.0 copy-done.2
  56.1 0.1 maximum_maximum_fusion.1
  56.2 0.6 copy.24
  57.0 0.0 copy-done.1
  57.0 0.0 copy-start.3
  57.0 0.2 maximum_maximum_fusion
  57.2 1.2 copy.25
  58.4 0.0 copy-done.3
  58.4 0.2 convert_reduce_fusion
  58.6 0.7 dynamic_slice.16.pick_ref
  59.7 0.1 scatter.161
  59.8 0.1 scatter.141
  60.0 0.1 scatter.164
  60.1 0.1 scatter.144
  60.2 0.1 scatter.121
  60.3 0.1 scatter.124
  60.7 0.1 compare_and_fusion
  60.8 0.7 constant_dynamic-update-slice_fusion.5
  61.5 0.7 constant_dynamic-update-slice_fusion.4
  62.2 0.7 constant_dynamic-update-slice_fusion.3
  62.9 0.7 constant_dynamic-update-slice_fusion.2
  63.6 0.7 constant_dynamic-update-slice_fusion.1
  64.2 0.7 constant_dynamic-update-slice_fusion.w_edge_ref
  64.9 8.8 %all-to-all-done = bf16[8,2,256,128]{3,2,1,0:T(8,128)(2,1)S(1)} async-done(((bf16[8,2,256,128]{3,2,1,0:T(8,128)(2,1)}), bf16[8,2,256,128]{3,2,1,0:T(8,128)(2,1)S(1)}, u32[]{:S(2)}, u32[]{:S(2)}) %all-to-all-start) | async-done | bytes 1048608 | tf_op jit(solution)/shard_map/all_to_all | solution.py:616
  73.7 0.0 copy-start
  73.7 0.6 gather_fusion
  74.4 0.1 broadcast_select_fusion
  74.5 3.6 %collective-permute-start = (bf16[8,256,128]{2,1,0:T(8,128)(2,1)S(1)}, bf16[8,256,128]{2,1,0:T(8,128)(2,1)S(1)}, u32[]{:S(2)}, u32[]{:S(2)}) collective-permute-start(bf16[8,256,128]{2,1,0:T(8,128)(2,1)S(1)} %broadcast_select_fusion), channel_id=1, source_target_pairs={{0,1},{1,0},{2,3},{3,2},{4,5},{5,4},{6,7},{7,6},{8,9},{9,8},{10,11... | collective-permute-start | bytes 1572872 | tf_op jit(solution)/shard_map/ppermute | solution.py:630
  78.1 0.6 compare_convert_fusion.own_ref
  78.7 0.0 collective-permute-done.1
  78.7 0.7 broadcast_select_fusion.2.left_ref
  79.3 0.0 collective-permute-done.2
  79.3 0.7 broadcast_select_fusion.1.right_ref
  80.0 0.0 collective-permute-done.far_ref
  80.0 0.0 copy-start.4
  80.0 0.0 copy-done
  80.0 0.8 copy-done.4
  80.8 50.5 %shard_map.110 = bf16[8,64,160,128]{3,2,1,0:T(8,128)(2,1)} custom-call(s32[8]{0:T(128)} %dynamic_slice.16.pick_ref, s32[8]{0:T(128)} %compare_convert_fusion.own_ref, bf16[16,256,128]{2,1,0:T(8,128)(2,1)} %bitcast.95, bf16[8,256,128]{2,1,0:T(8,128)(2,1)} %copy-done.4, bf16[8,64,128]{2,1,0:T(8,128)(2,1)} %broadcast_select_fusion.2.left_ref, ...), custom_call_target="tpu_custom_call" | custom-call | flops 33554432000 | bytes 41943040 | tf_op jit(solution)/shard_map/pallas_call | solution.py:196
  (46 shorter events, 1.0 us)
Async XLA Ops:
  42.7 13.2 %copy-start.2 = (bf16[3,3,128,3]{2,3,1,0:T(4,128)(2,1)S(1)}, bf16[3,3,128,3]{2,3,1,0:T(4,128)(2,1)}, u32[]{:S(2)}) copy-start(bf16[3,3,128,3]{2,3,1,0:T(4,128)(2,1)} %param.91) | copy-start | bytes 20740
  42.7 31.0 %all-to-all-start = ((bf16[8,2,256,128]{3,2,1,0:T(8,128)(2,1)}), bf16[8,2,256,128]{3,2,1,0:T(8,128)(2,1)S(1)}, u32[]{:S(2)}, u32[]{:S(2)}) async-start(bf16[8,2,256,128]{3,2,1,0:T(8,128)(2,1)} %shard_map.109), calls=%async_computation | async-start | bytes 2097152 | tf_op jit(solution)/shard_map/all_to_all | solution.py:616
  49.1 7.8 %copy-start.1 = (bf16[3,3,128,128]{3,2,1,0:T(8,128)(2,1)S(1)}, bf16[3,3,128,128]{3,2,1,0:T(8,128)(2,1)}, u32[]{:S(2)}) copy-start(bf16[3,3,128,128]{3,2,1,0:T(8,128)(2,1)} %param.92) | copy-start | bytes 884740
  51.2 27.5 %collective-permute-start.1 = (bf16[8,64,128]{2,1,0:T(8,128)(2,1)S(1)}, bf16[8,64,128]{2,1,0:T(8,128)(2,1)S(1)}, u32[]{:S(2)}, u32[]{:S(2)}) collective-permute-start(bf16[8,64,128]{2,1,0:T(8,128)(2,1)S(1)} %bitcast.98), channel_id=1, source_target_pairs={{0,2},{2,4},{4,6},{6,8},{8,10},{10,12},{12,14},{1,3},{3,5},{5,7},{... | collective-permute-start | bytes 393224 | tf_op jit(solution)/shard_map/ppermute | solution.py:620
  54.6 24.8 %collective-permute-start.2 = (bf16[8,64,128]{2,1,0:T(8,128)(2,1)S(1)}, bf16[8,64,128]{2,1,0:T(8,128)(2,1)S(1)}, u32[]{:S(2)}, u32[]{:S(2)}) collective-permute-start(bf16[8,64,128]{2,1,0:T(8,128)(2,1)S(1)} %bitcast.99), channel_id=1, source_target_pairs={{2,0},{4,2},{6,4},{8,6},{10,8},{12,10},{14,12},{3,1},{5,3},{7,5},{... | collective-permute-start | bytes 393224 | tf_op jit(solution)/shard_map/ppermute | solution.py:621
  57.0 1.4 %copy-start.3 = (s32[16]{0:T(128)S(1)}, s32[16]{0:T(128)}, u32[]{:S(2)}) copy-start(s32[16]{0:T(128)} %param.84) | copy-start | bytes 196
  73.7 6.3 %copy-start = (bf16[8,2,256,128]{3,2,1,0:T(8,128)(2,1)}, bf16[8,2,256,128]{3,2,1,0:T(8,128)(2,1)S(1)}, u32[]{:S(2)}) copy-start(bf16[8,2,256,128]{3,2,1,0:T(8,128)(2,1)S(1)} %all-to-all-done) | copy-start | bytes 3145732
  74.5 5.5 %collective-permute-start = (bf16[8,256,128]{2,1,0:T(8,128)(2,1)S(1)}, bf16[8,256,128]{2,1,0:T(8,128)(2,1)S(1)}, u32[]{:S(2)}, u32[]{:S(2)}) collective-permute-start(bf16[8,256,128]{2,1,0:T(8,128)(2,1)S(1)} %broadcast_select_fusion), channel_id=1, source_target_pairs={{0,1},{1,0},{2,3},{3,2},{4,5},{5,4},{6,7},{7,6},{8,9},{9,8},{10,11... | collective-permute-start | bytes 1572872 | tf_op jit(solution)/shard_map/ppermute | solution.py:630
  80.0 0.8 copy-start.4

commit v2 on v1

--- a/solution.py
+++ b/solution.py
@@ -30,8 +30,7 @@
     height,
     width,
     block_rows,
-    pick_ref,
-    own_ref,
+    code_ref,
     near_ref,
     far_ref,
     left_ref,
@@ -58,7 +57,7 @@
             grads_ref[s, 0] = zero_row
             grads_ref[s, height + 1] = zero_row
 
-    is_near = own_ref[frame] != 0
+    is_near = code_ref[frame] % 2 != 0
     message = jnp.where(is_near, near_ref[0].astype(jnp.float32), far_ref[0].astype(jnp.float32))
     mains = [message[k * height : (k + 1) * height] for k in range(3)]
     if rem > 0:
@@ -87,8 +86,13 @@
         + middle
         + jnp.concatenate([zeros, last[: height - 1]], axis=0)
     )
-    edge_ref[:, :LANES] = edge[:, :LANES] * silu_slope(left_ref[0].astype(jnp.float32))
-    edge_ref[:, LANES:] = edge[:, LANES:] * silu_slope(right_ref[0].astype(jnp.float32))
+    tile = lax.axis_index("tile")
+    has_left = jnp.where(tile > 0, 1.0, 0.0)
+    has_right = jnp.where(tile < lax.axis_size("tile") - 1, 1.0, 0.0)
+    left_slope = silu_slope(left_ref[0].astype(jnp.float32)) * has_left
+    right_slope = silu_slope(right_ref[0].astype(jnp.float32)) * has_right
+    edge_ref[:, :LANES] = edge[:, :LANES] * left_slope
+    edge_ref[:, LANES:] = edge[:, LANES:] * right_slope
 
     pairs = block_rows // 2
 
@@ -120,7 +124,6 @@
 
     def consume(block):
         base = block * block_rows
-        total = None
         slabs = []
         for j in range(4):
             for s in range(3):
@@ -128,7 +131,9 @@
                     jnp.concatenate([grads_ref[s, base + 2 * p + j] for p in range(pairs)], axis=0)
                 )
         lhs = jnp.concatenate(slabs, axis=1)
-        total = jnp.dot(lhs, w_two_ref[...], preferred_element_type=jnp.float32)
+        half = lhs.shape[1] // 2
+        total = jnp.dot(lhs[:, :half], w_two_ref[:half], preferred_element_type=jnp.float32)
+        total += jnp.dot(lhs[:, half:], w_two_ref[half:], preferred_element_type=jnp.float32)
         for i in range(block_rows):
             p, h = i // 2, i % 2
             part = total[p * width : (p + 1) * width, h * LANES : (h + 1) * LANES]
@@ -187,21 +192,21 @@
     return w_edge, w_one, w_two
 
 
-def decode(pick, own, near, far, left, right, activations, conv_out_weight, conv_weight, block_rows):
+def decode(code, near, far, left, right, activations, weights, block_rows):
     frames, height, width, channels = activations.shape
     rows = near.shape[1]
-    w_edge, w_one, w_two = decoder_weights(conv_out_weight, conv_weight, height, width)
+    w_edge, w_one, w_two = weights
     whole = lambda shape: pl.BlockSpec(shape, lambda f, *_: (0,) * len(shape))
     padded = -(-(width + 9) // 8) * 8 + 8
     return pl.pallas_call(
         functools.partial(decoder_kernel, height, width, block_rows),
         out_shape=jax.ShapeDtypeStruct(activations.shape, jnp.bfloat16),
         grid_spec=pltpu.PrefetchScalarGridSpec(
-            num_scalar_prefetch=2,
+            num_scalar_prefetch=1,
             grid=(frames,),
             in_specs=[
-                pl.BlockSpec((1, rows, LANES), lambda f, pick, own: (pick[f], 0, 0)),
-                pl.BlockSpec((1, rows, LANES), lambda f, pick, own: (f, 0, 0)),
+                pl.BlockSpec((1, rows, LANES), lambda f, code: (code[f] // 2, 0, 0)),
+                pl.BlockSpec((1, rows, LANES), lambda f, code: (f, 0, 0)),
                 pl.BlockSpec((1, height, channels), lambda f, *_: (f, 0, 0)),
                 pl.BlockSpec((1, height, channels), lambda f, *_: (f, 0, 0)),
                 pl.BlockSpec((1, height, width, channels), lambda f, *_: (f, 0, 0, 0)),
@@ -223,7 +228,7 @@
             bytes_accessed=4 * frames * height * width * channels,
             transcendentals=frames * height * width * channels,
         ),
-    )(pick, own, near, far, left, right, activations, w_edge, w_one, w_two)
+    )(code, near, far, left, right, activations, w_edge, w_one, w_two)
 
 
 def dot(left, right, dims=((1,), (0,))):
@@ -297,8 +302,11 @@
         at = slice(n * block, (n + 1) * block)
         patch_ref[:, at] = dot(move, patch_raw_ref[:, at]).astype(NARROW)
 
+    every = dot(
+        jnp.concatenate([pixel_ref[f] for f in range(slots)], axis=0), order_ref[...]
+    )
     for f in range(slots):
-        spread = dot(pixel_ref[f], order_ref[...])
+        spread = every[f * colour_rows : (f + 1) * colour_rows]
         for py in range(down):
             entries = jnp.concatenate(
                 [
@@ -362,15 +370,15 @@
         key_at = pl.ds(pl.multiple_of(dim + i * LANES, LANES), LANES)
         return rows, query_at, key_at
 
-    @pl.loop(0, slots * pairs, unroll=16)
+    @pl.loop(0, slots * pairs, unroll=8)
     def _(index):
         rows, query_at, key_at = pair_at(index)
         query = heads_ref[rows, query_at]
         key = heads_ref[rows, key_at]
+        masks = [jnp.where(side, factor, 0.0).astype(NARROW) for side in sides]
+        both = dot_rows(jnp.concatenate([query * mask for mask in masks], axis=0), key)
         for side in range(2):
-            mask = jnp.where(sides[side], factor, 0.0).astype(NARROW)
-            scores = dot_rows(query * mask, key)
-            exps = jnp.exp(scores)
+            exps = jnp.exp(both[side * tokens : (side + 1) * tokens])
             probs = exps * (1.0 / jnp.sum(exps, axis=1, keepdims=True))
             column_ref[pl.ds(2 * index + side, 1), :] = jnp.sum(probs, axis=0, keepdims=True)
             probs_ref[2 * index + side] = probs.astype(NARROW)
@@ -430,23 +438,25 @@
             value_back[f * HEADS : (f + 1) * HEADS], normed[f]
         )
 
-    @pl.loop(0, slots * pairs, unroll=16)
+    @pl.loop(0, slots * pairs, unroll=8)
     def _(index):
         rows, query_at, key_at = pair_at(index)
         query = heads_ref[rows, query_at]
         key = heads_ref[rows, key_at]
-        query_back, key_back = [], []
+        scores_back = []
         for side in range(2):
             probs = probs_ref[2 * index + side].astype(WIDE)
             slope = slope_ref[pl.ds(2 * index + side, 1), :]
             middle = jnp.sum(probs * slope, axis=1, keepdims=True)
-            scores_back = (probs * (slope - middle)).astype(NARROW)
-            query_back.append(dot(scores_back, key))
-            key_back.append(dot(scores_back, query, ((0,), (0,))))
+            scores_back.append((probs * (slope - middle)).astype(NARROW))
+        query_back = dot(jnp.concatenate(scores_back, axis=0), key)
+        key_back = jnp.concatenate(
+            [dot(part, query, ((0,), (0,))) for part in scores_back], axis=0
+        )
         gradient = jnp.concatenate(
             [
-                jnp.where(sides[0], query_back[0], query_back[1]),
-                jnp.where(sides[0], key_back[0], key_back[1]),
+                jnp.where(sides[0], query_back[:tokens], query_back[tokens:]),
+                jnp.where(sides[0], key_back[:tokens], key_back[tokens:]),
             ],
             axis=1,
         )
@@ -481,11 +491,11 @@
         value = scale_ref[rows, :1] * value + token_back[8 * f : 8 * f + 1]
         tangent_ref[b * LANES : b * LANES + across, :] = value.astype(NARROW)
 
+    lines = []
     for f in range(slots):
         entries = dot_rows(
             patch_ref[...], tangent_ref[f * down * LANES : (f + 1) * down * LANES, :]
         ).astype(NARROW)
-        lines = []
         for k in range(3):
             for py in range(down):
                 lines.append(
@@ -500,7 +510,9 @@
                         axis=1,
                     )
                 )
-        frame = dot_rows(jnp.concatenate(lines, axis=0), order_ref[...])
+    every = dot_rows(jnp.concatenate(lines, axis=0), order_ref[...])
+    for f in range(slots):
+        frame = every[f * colour_rows : (f + 1) * colour_rows]
         frame = jnp.concatenate(
             [
                 jnp.zeros((colour_rows, 2), WIDE),
@@ -603,7 +615,6 @@
     tile_count = lax.axis_size("tile")
     core_count = lax.axis_size("tm")
     core = lax.axis_index("tm")
-    tile = lax.axis_index("tile")
     frames, height, width, channels = activations.shape
     slots = pixels.shape[0]
     ranks_all = frame_rank(owner)
@@ -616,28 +627,28 @@
     near = lax.all_to_all(outgoing, "tile", split_axis=0, concat_axis=0, tiled=True)
     up = [(i, i + 1) for i in range(tile_count - 1)]
     down = [(j, i) for i, j in up]
-    outside = jnp.asarray(-30000.0, activations.dtype)
     left = lax.ppermute(lax.dynamic_index_in_dim(activations, origin + (width - 1), 2, False), "tile", up)
     right = lax.ppermute(lax.dynamic_index_in_dim(activations, origin, 2, False), "tile", down)
-    left = jnp.where(tile == 0, outside, left)
-    right = jnp.where(tile == tile_count - 1, outside, right)
 
     near = near.reshape(tile_count * slots, rows, LANES)
     pick_all = (owner // core_count) * slots + ranks_all
-    own_all = owner % core_count
+    code_all = 2 * pick_all + (owner % core_count == core).astype(jnp.int32)
     by_core = lambda values, index: lax.dynamic_slice_in_dim(values, index * frames, frames)
+    code = by_core(code_all, core)
+    weights = decoder_weights(conv_out_weight, conv_weight, height, width)
+    near, code, left, right, *weights = lax.optimization_barrier(
+        (near, code, left, right, *weights)
+    )
     other = 1 - core
     far = lax.ppermute(jnp.take(near, by_core(pick_all, other), axis=0), "tm", [(0, 1), (1, 0)])
     return decode(
-        by_core(pick_all, core),
-        (by_core(own_all, core) == core).astype(jnp.int32),
+        code,
         near,
         far,
         left,
         right,
         activations,
-        conv_out_weight,
-        conv_weight,
+        weights,
         4,
     )
 

time: 132 us -> 130 us (0.985)
  waiting for transfers between devices: 8.81 us -> 14 us
  local copies, waits for them, and re-layouts: 11.8 us -> 7.9 us
  other arithmetic: 2.6 us -> 0.69 us
  Pallas kernels: 93.2 us -> 91.7 us
    unnamed x18 -> x24, local copies, waits for them, and re-layouts: 4.32 us -> 1.03 us
    all_to_all x1, waiting for transfers between devices: 8.8 us -> 10.8 us  [local(): lax.all_to_all(outgoing, 'tile', split_axis=0, concat_axis=0, tiled=True)]
    ppermute x1, waiting for transfers between devices: 0.01 us -> 1.54 us  [local(): lax.ppermute(jnp.take(near, by_core(pick_all, other), axis=0), 'tm', [(0,...]
    select_n x3 -> x0, other arithmetic: 1.34 us -> none  [the longest x1 0.67 us: local(): left = jnp.where(tile == 0, outside, left)]
  transfers between devices with their start and end apart: 4 -> 4, of which waited for: 1 -> 4; matrix products, arithmetic and copies ran while one was open for 10% -> 5% of each run, Pallas kernels for 0% -> 0%
where the time goes in v2:
time: 130 us; the launch traced here: 129 us
  Pallas kernels  91.7 us (71%)
  starting transfers between devices  14.8 us (11%)
  waiting for transfers between devices  14 us (11%)
  local copies, waits for them, and re-layouts  7.9 us (6%)
    pallas_call x1, Pallas kernels, decode(): pl.pallas_call(functools.partial(decoder_kernel, height, width, block_row...  49.5 us
    pallas_call x1, Pallas kernels, tower(): pl.pallas_call(functools.partial(tower_kernel, tiles), out_shape=jax.Shap...  42.2 us
    all_to_all x1, waiting for transfers between devices, local(): lax.all_to_all(outgoing, 'tile', split_axis=0, concat_axis=0, tiled=True)  10.8 us
    all_to_all x1, starting transfers between devices, local(): lax.all_to_all(outgoing, 'tile', split_axis=0, concat_axis=0, tiled=True)  6.4 us
    ppermute x1, starting transfers between devices, local(): lax.ppermute(jnp.take(near, by_core(pick_all, other), axis=0), 'tm', [(0,...  3.59 us
    ppermute x1, starting transfers between devices, local(): lax.ppermute(lax.dynamic_index_in_dim(activations, origin + (width - 1),...  3.5 us
  transfers between devices with their start and end apart: 4, of which 4 were waited for; matrix products, arithmetic and copies ran while one was open for 5% of the time, Pallas kernels for 0%

profile of v2, /device:TPU:1, one launch (start us, length us, event | category | flops | bytes accessed | tf_op | source)
XLA Modules:
  0.0 129.5 jit_solution(12572431503039025517)
XLA Ops:
  0.0 42.2 %shard_map.109 = bf16[8,2,256,128]{3,2,1,0:T(8,128)(2,1)} custom-call(bf16[2,192,1280]{2,1,0:T(8,128)(2,1)} %bitcast.103, bf16[768,1024]{1,0:T(8,128)(2,1)} %patch_raw_ref.1, f32[1,1024]{1,0:T(1,128)} %bitcast.104, bf16[1024,3072]{1,0:T(8,128)(2,1)} %qkv_ref.1, bf16[1024,1024]{1,0:T(8,128)(2,1)} %proj_ref.1, f32[1,1024]{1,0:T(1,128)} %bitcast.105, ...), custom_call_target="tpu_custom_call" | custom-call | flops 9059696640 | bytes 9961472 | tf_op jit(solution)/shard_map/pallas_call | solution.py:554
  42.3 0.0 copy-start.2
  42.3 6.4 %all-to-all-start = ((bf16[8,2,256,128]{3,2,1,0:T(8,128)(2,1)}), bf16[8,2,256,128]{3,2,1,0:T(8,128)(2,1)S(1)}, u32[]{:S(2)}, u32[]{:S(2)}) async-start(bf16[8,2,256,128]{3,2,1,0:T(8,128)(2,1)} %shard_map.109), calls=%async_computation | async-start | bytes 2097152 | tf_op jit(solution)/shard_map/all_to_all | solution.py:627
  48.7 0.0 copy-start.4
  48.7 2.1 %constant_dynamic-slice_fusion = (bf16[8,64,1,128]{3,2,1,0:T(2,128)(2,1)S(1)}, bf16[8,64,1,128]{3,2,1,0:T(2,128)(2,1)S(1)}) fusion(bf16[8,64,160,128]{3,2,1,0:T(8,128)(2,1)} %act_ref.1, s32[]{:T(128)S(6)} %select_n.38, s32[]{:T(128)S(6)} %select_n.37), kind=kLoop, calls=%fused_computation.68 | loop fusion | bytes 524296 | tf_op jit(solution)/shard_map/jit(dynamic_index_in_dim)/dynamic_slice | solution.py:631
  50.8 0.0 copy-start.1
  50.8 3.5 %collective-permute-start = (bf16[8,64,128]{2,1,0:T(8,128)(2,1)S(1)}, bf16[8,64,128]{2,1,0:T(8,128)(2,1)S(1)}, u32[]{:S(2)}, u32[]{:S(2)}) collective-permute-start(bf16[8,64,128]{2,1,0:T(8,128)(2,1)S(1)} %bitcast.98), channel_id=1, source_target_pairs={{0,2},{2,4},{4,6},{6,8},{8,10},{10,12},{12,14},{1,3},{3,5},{5,7},{... | collective-permute-start | bytes 393224 | tf_op jit(solution)/shard_map/ppermute | solution.py:630
  54.3 1.3 collective-permute-start.1
  55.6 0.0 copy-done.2
  56.0 0.1 scatter.161
  56.1 0.1 scatter.141
  56.2 0.1 scatter.164
  56.3 0.1 scatter.144
  56.4 0.1 scatter.121
  56.6 0.1 scatter.124
  57.1 0.0 copy-done.4
  57.2 0.2 convert_reduce_fusion
  57.4 0.1 compare_and_fusion
  57.5 0.1 maximum_maximum_fusion.1
  57.8 0.0 copy-done.1
  57.8 0.2 maximum_maximum_fusion
  58.0 0.6 copy.24
  58.7 1.2 copy.25
  59.9 0.7 dynamic_slice.13.code_ref
  60.8 0.0 copy-start.3
  60.8 0.6 collective-permute-done.left_ref
  61.4 0.0 copy-start.6
  61.4 1.1 collective-permute-done.1.right_ref
  62.5 0.0 copy-start.7
  62.5 10.8 %all-to-all-done = bf16[8,2,256,128]{3,2,1,0:T(8,128)(2,1)S(1)} async-done(((bf16[8,2,256,128]{3,2,1,0:T(8,128)(2,1)}), bf16[8,2,256,128]{3,2,1,0:T(8,128)(2,1)S(1)}, u32[]{:S(2)}, u32[]{:S(2)}) %all-to-all-start) | async-done | bytes 1048608 | tf_op jit(solution)/shard_map/all_to_all | solution.py:627
  73.3 0.0 copy-start
  73.3 0.6 gather_fusion
  73.9 0.1 broadcast_select_fusion
  74.1 3.6 %collective-permute-start.2 = (bf16[8,256,128]{2,1,0:T(8,128)(2,1)S(1)}, bf16[8,256,128]{2,1,0:T(8,128)(2,1)S(1)}, u32[]{:S(2)}, u32[]{:S(2)}) collective-permute-start(bf16[8,256,128]{2,1,0:T(8,128)(2,1)S(1)} %broadcast_select_fusion), channel_id=1, source_target_pairs={{0,1},{1,0},{2,3},{3,2},{4,5},{5,4},{6,7},{7,6},{8,9},{9,8},{10,11... | collective-permute-start | bytes 1572872 | tf_op jit(solution)/shard_map/ppermute | solution.py:643
  77.6 1.5 %collective-permute-done.2.far_ref = bf16[8,256,128]{2,1,0:T(8,128)(2,1)S(1)} collective-permute-done((bf16[8,256,128]{2,1,0:T(8,128)(2,1)S(1)}, bf16[8,256,128]{2,1,0:T(8,128)(2,1)S(1)}, u32[]{:S(2)}, u32[]{:S(2)}) %collective-permute-start.2) | collective-permute-done | bytes 524320 | tf_op jit(solution)/shard_map/ppermute | solution.py:643
  79.2 0.0 copy-done.3
  79.2 0.0 copy-done.6
  79.2 0.0 copy-done.7
  79.2 0.0 copy-done
  79.2 0.0 copy-start.5
  79.2 0.8 copy-done.5
  80.0 49.5 %shard_map.110 = bf16[8,64,160,128]{3,2,1,0:T(8,128)(2,1)} custom-call(s32[8]{0:T(128)} %dynamic_slice.13.code_ref, bf16[16,256,128]{2,1,0:T(8,128)(2,1)} %bitcast.95, bf16[8,256,128]{2,1,0:T(8,128)(2,1)} %copy-done.5, bf16[8,64,128]{2,1,0:T(8,128)(2,1)} %copy-done.6, bf16[8,64,128]{2,1,0:T(8,128)(2,1)} %copy-done.7, bf16[8,64,160,128]{3,2,1,0:T(8,128)(2,1)} %act_ref.1, ...), custom_call_target="tpu_custom_call" | custom-call | flops 33554432000 | bytes 41943040 | tf_op jit(solution)/shard_map/pallas_call | solution.py:201
  (52 shorter events, 1.2 us)
Async XLA Ops:
  42.3 13.4 %copy-start.2 = (bf16[3,3,128,3]{2,3,1,0:T(4,128)(2,1)S(1)}, bf16[3,3,128,3]{2,3,1,0:T(4,128)(2,1)}, u32[]{:S(2)}) copy-start(bf16[3,3,128,3]{2,3,1,0:T(4,128)(2,1)} %param.91) | copy-start | bytes 20740
  42.3 31.0 %all-to-all-start = ((bf16[8,2,256,128]{3,2,1,0:T(8,128)(2,1)}), bf16[8,2,256,128]{3,2,1,0:T(8,128)(2,1)S(1)}, u32[]{:S(2)}, u32[]{:S(2)}) async-start(bf16[8,2,256,128]{3,2,1,0:T(8,128)(2,1)} %shard_map.109), calls=%async_computation | async-start | bytes 2097152 | tf_op jit(solution)/shard_map/all_to_all | solution.py:627
  48.7 8.5 %copy-start.4 = (s32[16]{0:T(128)S(1)}, s32[16]{0:T(128)}, u32[]{:S(2)}) copy-start(s32[16]{0:T(128)} %param.84) | copy-start | bytes 196
  50.8 7.0 %copy-start.1 = (bf16[3,3,128,128]{3,2,1,0:T(8,128)(2,1)S(1)}, bf16[3,3,128,128]{3,2,1,0:T(8,128)(2,1)}, u32[]{:S(2)}) copy-start(bf16[3,3,128,128]{3,2,1,0:T(8,128)(2,1)} %param.92) | copy-start | bytes 884740
  50.8 10.6 %collective-permute-start = (bf16[8,64,128]{2,1,0:T(8,128)(2,1)S(1)}, bf16[8,64,128]{2,1,0:T(8,128)(2,1)S(1)}, u32[]{:S(2)}, u32[]{:S(2)}) collective-permute-start(bf16[8,64,128]{2,1,0:T(8,128)(2,1)S(1)} %bitcast.98), channel_id=1, source_target_pairs={{0,2},{2,4},{4,6},{6,8},{8,10},{10,12},{12,14},{1,3},{3,5},{5,7},{... | collective-permute-start | bytes 393224 | tf_op jit(solution)/shard_map/ppermute | solution.py:630
  54.3 8.1 %collective-permute-start.1 = (bf16[8,64,128]{2,1,0:T(8,128)(2,1)S(1)}, bf16[8,64,128]{2,1,0:T(8,128)(2,1)S(1)}, u32[]{:S(2)}, u32[]{:S(2)}) collective-permute-start(bf16[8,64,128]{2,1,0:T(8,128)(2,1)S(1)} %bitcast.99), channel_id=1, source_target_pairs={{2,0},{4,2},{6,4},{8,6},{10,8},{12,10},{14,12},{3,1},{5,3},{7,5},{... | collective-permute-start | bytes 393224 | tf_op jit(solution)/shard_map/ppermute | solution.py:631
  60.8 18.4 %copy-start.3 = (bf16[512,768]{1,0:T(8,128)(2,1)}, bf16[512,768]{1,0:T(8,128)(2,1)S(1)}, u32[]{:S(2)}) copy-start(bf16[512,768]{1,0:T(8,128)(2,1)S(1)} %constant_dynamic-update-slice_fusion.w_edge_ref) | copy-start | bytes 2359300
  61.4 17.8 %copy-start.6 = (bf16[8,64,128]{2,1,0:T(8,128)(2,1)}, bf16[8,64,128]{2,1,0:T(8,128)(2,1)S(1)}, u32[]{:S(2)}) copy-start(bf16[8,64,128]{2,1,0:T(8,128)(2,1)S(1)} %collective-permute-done.left_ref) | copy-start | bytes 393220
  62.5 16.7 %copy-start.7 = (bf16[8,64,128]{2,1,0:T(8,128)(2,1)}, bf16[8,64,128]{2,1,0:T(8,128)(2,1)S(1)}, u32[]{:S(2)}) copy-start(bf16[8,64,128]{2,1,0:T(8,128)(2,1)S(1)} %collective-permute-done.1.right_ref) | copy-start | bytes 393220
  73.3 5.9 %copy-start = (bf16[8,2,256,128]{3,2,1,0:T(8,128)(2,1)}, bf16[8,2,256,128]{3,2,1,0:T(8,128)(2,1)S(1)}, u32[]{:S(2)}) copy-start(bf16[8,2,256,128]{3,2,1,0:T(8,128)(2,1)S(1)} %all-to-all-done) | copy-start | bytes 3145732
  74.1 5.1 %collective-permute-start.2 = (bf16[8,256,128]{2,1,0:T(8,128)(2,1)S(1)}, bf16[8,256,128]{2,1,0:T(8,128)(2,1)S(1)}, u32[]{:S(2)}, u32[]{:S(2)}) collective-permute-start(bf16[8,256,128]{2,1,0:T(8,128)(2,1)S(1)} %broadcast_select_fusion), channel_id=1, source_target_pairs={{0,1},{1,0},{2,3},{3,2},{4,5},{5,4},{6,7},{7,6},{8,9},{9,8},{10,11... | collective-permute-start | bytes 1572872 | tf_op jit(solution)/shard_map/ppermute | solution.py:643
  79.2 0.8 copy-start.5

commit v3 on v2

--- a/solution.py
+++ b/solution.py
@@ -438,7 +438,7 @@
             value_back[f * HEADS : (f + 1) * HEADS], normed[f]
         )
 
-    @pl.loop(0, slots * pairs, unroll=8)
+    @pl.loop(0, slots * pairs, unroll=16)
     def _(index):
         rows, query_at, key_at = pair_at(index)
         query = heads_ref[rows, query_at]

time: 130 us -> 130 us (level)
  no operation moved by 1% of the time
where the time goes in v3:
time: 130 us; the launch traced here: 129 us
  Pallas kernels  91.6 us (70%)
  starting transfers between devices  14.8 us (11%)
  waiting for transfers between devices  14 us (11%)
  local copies, waits for them, and re-layouts  7.9 us (6%)
    pallas_call x1, Pallas kernels, decode(): pl.pallas_call(functools.partial(decoder_kernel, height, width, block_row...  49.5 us
    pallas_call x1, Pallas kernels, tower(): pl.pallas_call(functools.partial(tower_kernel, tiles), out_shape=jax.Shap...  42.1 us
    all_to_all x1, waiting for transfers between devices, local(): lax.all_to_all(outgoing, 'tile', split_axis=0, concat_axis=0, tiled=True)  10.8 us
    all_to_all x1, starting transfers between devices, local(): lax.all_to_all(outgoing, 'tile', split_axis=0, concat_axis=0, tiled=True)  6.4 us
    ppermute x1, starting transfers between devices, local(): lax.ppermute(jnp.take(near, by_core(pick_all, other), axis=0), 'tm', [(0,...  3.59 us
    ppermute x1, starting transfers between devices, local(): lax.ppermute(lax.dynamic_index_in_dim(activations, origin + (width - 1),...  3.5 us
  transfers between devices with their start and end apart: 4, of which 4 were waited for; matrix products, arithmetic and copies ran while one was open for 5% of the time, Pallas kernels for 0%

profile of v3, /device:TPU:1, one launch (start us, length us, event | category | flops | bytes accessed | tf_op | source)
XLA Modules:
  0.0 129.3 jit_solution(1830253006842970020)
XLA Ops:
  0.0 42.1 %shard_map.109 = bf16[8,2,256,128]{3,2,1,0:T(8,128)(2,1)} custom-call(bf16[2,192,1280]{2,1,0:T(8,128)(2,1)} %bitcast.103, bf16[768,1024]{1,0:T(8,128)(2,1)} %patch_raw_ref.1, f32[1,1024]{1,0:T(1,128)} %bitcast.104, bf16[1024,3072]{1,0:T(8,128)(2,1)} %qkv_ref.1, bf16[1024,1024]{1,0:T(8,128)(2,1)} %proj_ref.1, f32[1,1024]{1,0:T(1,128)} %bitcast.105, ...), custom_call_target="tpu_custom_call" | custom-call | flops 9059696640 | bytes 9961472 | tf_op jit(solution)/shard_map/pallas_call | solution.py:554
  42.1 0.0 copy-start.2
  42.1 6.4 %all-to-all-start = ((bf16[8,2,256,128]{3,2,1,0:T(8,128)(2,1)}), bf16[8,2,256,128]{3,2,1,0:T(8,128)(2,1)S(1)}, u32[]{:S(2)}, u32[]{:S(2)}) async-start(bf16[8,2,256,128]{3,2,1,0:T(8,128)(2,1)} %shard_map.109), calls=%async_computation | async-start | bytes 2097152 | tf_op jit(solution)/shard_map/all_to_all | solution.py:627
  48.5 0.0 copy-start.4
  48.5 2.1 %constant_dynamic-slice_fusion = (bf16[8,64,1,128]{3,2,1,0:T(2,128)(2,1)S(1)}, bf16[8,64,1,128]{3,2,1,0:T(2,128)(2,1)S(1)}) fusion(bf16[8,64,160,128]{3,2,1,0:T(8,128)(2,1)} %act_ref.1, s32[]{:T(128)S(6)} %select_n.38, s32[]{:T(128)S(6)} %select_n.37), kind=kLoop, calls=%fused_computation.68 | loop fusion | bytes 524296 | tf_op jit(solution)/shard_map/jit(dynamic_index_in_dim)/dynamic_slice | solution.py:631
  50.6 0.0 copy-start.1
  50.7 3.5 %collective-permute-start = (bf16[8,64,128]{2,1,0:T(8,128)(2,1)S(1)}, bf16[8,64,128]{2,1,0:T(8,128)(2,1)S(1)}, u32[]{:S(2)}, u32[]{:S(2)}) collective-permute-start(bf16[8,64,128]{2,1,0:T(8,128)(2,1)S(1)} %bitcast.98), channel_id=1, source_target_pairs={{0,2},{2,4},{4,6},{6,8},{8,10},{10,12},{12,14},{1,3},{3,5},{5,7},{... | collective-permute-start | bytes 393224 | tf_op jit(solution)/shard_map/ppermute | solution.py:630
  54.2 1.3 collective-permute-start.1
  55.5 0.0 copy-done.2
  55.8 0.1 scatter.161
  55.9 0.1 scatter.141
  56.1 0.1 scatter.164
  56.2 0.1 scatter.144
  56.3 0.1 scatter.121
  56.4 0.1 scatter.124
  57.0 0.0 copy-done.4
  57.0 0.2 convert_reduce_fusion
  57.2 0.1 compare_and_fusion
  57.3 0.1 maximum_maximum_fusion.1
  57.6 0.0 copy-done.1
  57.7 0.2 maximum_maximum_fusion
  57.9 0.6 copy.24
  58.5 1.2 copy.25
  59.7 0.7 dynamic_slice.13.code_ref
  60.7 0.0 copy-start.3
  60.7 0.6 collective-permute-done.left_ref
  61.2 0.0 copy-start.6
  61.3 1.1 collective-permute-done.1.right_ref
  62.3 0.0 copy-start.7
  62.3 10.8 %all-to-all-done = bf16[8,2,256,128]{3,2,1,0:T(8,128)(2,1)S(1)} async-done(((bf16[8,2,256,128]{3,2,1,0:T(8,128)(2,1)}), bf16[8,2,256,128]{3,2,1,0:T(8,128)(2,1)S(1)}, u32[]{:S(2)}, u32[]{:S(2)}) %all-to-all-start) | async-done | bytes 1048608 | tf_op jit(solution)/shard_map/all_to_all | solution.py:627
  73.1 0.0 copy-start
  73.1 0.6 gather_fusion
  73.8 0.1 broadcast_select_fusion
  73.9 3.6 %collective-permute-start.2 = (bf16[8,256,128]{2,1,0:T(8,128)(2,1)S(1)}, bf16[8,256,128]{2,1,0:T(8,128)(2,1)S(1)}, u32[]{:S(2)}, u32[]{:S(2)}) collective-permute-start(bf16[8,256,128]{2,1,0:T(8,128)(2,1)S(1)} %broadcast_select_fusion), channel_id=1, source_target_pairs={{0,1},{1,0},{2,3},{3,2},{4,5},{5,4},{6,7},{7,6},{8,9},{9,8},{10,11... | collective-permute-start | bytes 1572872 | tf_op jit(solution)/shard_map/ppermute | solution.py:643
  77.5 1.5 %collective-permute-done.2.far_ref = bf16[8,256,128]{2,1,0:T(8,128)(2,1)S(1)} collective-permute-done((bf16[8,256,128]{2,1,0:T(8,128)(2,1)S(1)}, bf16[8,256,128]{2,1,0:T(8,128)(2,1)S(1)}, u32[]{:S(2)}, u32[]{:S(2)}) %collective-permute-start.2) | collective-permute-done | bytes 524320 | tf_op jit(solution)/shard_map/ppermute | solution.py:643
  79.0 0.0 copy-done.3
  79.0 0.0 copy-done.6
  79.1 0.0 copy-done.7
  79.1 0.0 copy-done
  79.1 0.0 copy-start.5
  79.1 0.8 copy-done.5
  79.9 49.5 %shard_map.110 = bf16[8,64,160,128]{3,2,1,0:T(8,128)(2,1)} custom-call(s32[8]{0:T(128)} %dynamic_slice.13.code_ref, bf16[16,256,128]{2,1,0:T(8,128)(2,1)} %bitcast.95, bf16[8,256,128]{2,1,0:T(8,128)(2,1)} %copy-done.5, bf16[8,64,128]{2,1,0:T(8,128)(2,1)} %copy-done.6, bf16[8,64,128]{2,1,0:T(8,128)(2,1)} %copy-done.7, bf16[8,64,160,128]{3,2,1,0:T(8,128)(2,1)} %act_ref.1, ...), custom_call_target="tpu_custom_call" | custom-call | flops 33554432000 | bytes 41943040 | tf_op jit(solution)/shard_map/pallas_call | solution.py:201
  (52 shorter events, 1.2 us)
Async XLA Ops:
  42.1 13.4 %copy-start.2 = (bf16[3,3,128,3]{2,3,1,0:T(4,128)(2,1)S(1)}, bf16[3,3,128,3]{2,3,1,0:T(4,128)(2,1)}, u32[]{:S(2)}) copy-start(bf16[3,3,128,3]{2,3,1,0:T(4,128)(2,1)} %param.91) | copy-start | bytes 20740
  42.1 31.0 %all-to-all-start = ((bf16[8,2,256,128]{3,2,1,0:T(8,128)(2,1)}), bf16[8,2,256,128]{3,2,1,0:T(8,128)(2,1)S(1)}, u32[]{:S(2)}, u32[]{:S(2)}) async-start(bf16[8,2,256,128]{3,2,1,0:T(8,128)(2,1)} %shard_map.109), calls=%async_computation | async-start | bytes 2097152 | tf_op jit(solution)/shard_map/all_to_all | solution.py:627
  48.5 8.5 %copy-start.4 = (s32[16]{0:T(128)S(1)}, s32[16]{0:T(128)}, u32[]{:S(2)}) copy-start(s32[16]{0:T(128)} %param.84) | copy-start | bytes 196
  50.6 7.0 %copy-start.1 = (bf16[3,3,128,128]{3,2,1,0:T(8,128)(2,1)S(1)}, bf16[3,3,128,128]{3,2,1,0:T(8,128)(2,1)}, u32[]{:S(2)}) copy-start(bf16[3,3,128,128]{3,2,1,0:T(8,128)(2,1)} %param.92) | copy-start | bytes 884740
  50.7 10.6 %collective-permute-start = (bf16[8,64,128]{2,1,0:T(8,128)(2,1)S(1)}, bf16[8,64,128]{2,1,0:T(8,128)(2,1)S(1)}, u32[]{:S(2)}, u32[]{:S(2)}) collective-permute-start(bf16[8,64,128]{2,1,0:T(8,128)(2,1)S(1)} %bitcast.98), channel_id=1, source_target_pairs={{0,2},{2,4},{4,6},{6,8},{8,10},{10,12},{12,14},{1,3},{3,5},{5,7},{... | collective-permute-start | bytes 393224 | tf_op jit(solution)/shard_map/ppermute | solution.py:630
  54.2 8.1 %collective-permute-start.1 = (bf16[8,64,128]{2,1,0:T(8,128)(2,1)S(1)}, bf16[8,64,128]{2,1,0:T(8,128)(2,1)S(1)}, u32[]{:S(2)}, u32[]{:S(2)}) collective-permute-start(bf16[8,64,128]{2,1,0:T(8,128)(2,1)S(1)} %bitcast.99), channel_id=1, source_target_pairs={{2,0},{4,2},{6,4},{8,6},{10,8},{12,10},{14,12},{3,1},{5,3},{7,5},{... | collective-permute-start | bytes 393224 | tf_op jit(solution)/shard_map/ppermute | solution.py:631
  60.7 18.4 %copy-start.3 = (bf16[512,768]{1,0:T(8,128)(2,1)}, bf16[512,768]{1,0:T(8,128)(2,1)S(1)}, u32[]{:S(2)}) copy-start(bf16[512,768]{1,0:T(8,128)(2,1)S(1)} %constant_dynamic-update-slice_fusion.w_edge_ref) | copy-start | bytes 2359300
  61.2 17.8 %copy-start.6 = (bf16[8,64,128]{2,1,0:T(8,128)(2,1)}, bf16[8,64,128]{2,1,0:T(8,128)(2,1)S(1)}, u32[]{:S(2)}) copy-start(bf16[8,64,128]{2,1,0:T(8,128)(2,1)S(1)} %collective-permute-done.left_ref) | copy-start | bytes 393220
  62.3 16.7 %copy-start.7 = (bf16[8,64,128]{2,1,0:T(8,128)(2,1)}, bf16[8,64,128]{2,1,0:T(8,128)(2,1)S(1)}, u32[]{:S(2)}) copy-start(bf16[8,64,128]{2,1,0:T(8,128)(2,1)S(1)} %collective-permute-done.1.right_ref) | copy-start | bytes 393220
  73.1 5.9 %copy-start = (bf16[8,2,256,128]{3,2,1,0:T(8,128)(2,1)}, bf16[8,2,256,128]{3,2,1,0:T(8,128)(2,1)S(1)}, u32[]{:S(2)}) copy-start(bf16[8,2,256,128]{3,2,1,0:T(8,128)(2,1)S(1)} %all-to-all-done) | copy-start | bytes 3145732
  73.9 5.1 %collective-permute-start.2 = (bf16[8,256,128]{2,1,0:T(8,128)(2,1)S(1)}, bf16[8,256,128]{2,1,0:T(8,128)(2,1)S(1)}, u32[]{:S(2)}, u32[]{:S(2)}) collective-permute-start(bf16[8,256,128]{2,1,0:T(8,128)(2,1)S(1)} %broadcast_select_fusion), channel_id=1, source_target_pairs={{0,1},{1,0},{2,3},{3,2},{4,5},{5,4},{6,7},{7,6},{8,9},{9,8},{10,11... | collective-permute-start | bytes 1572872 | tf_op jit(solution)/shard_map/ppermute | solution.py:643
  79.1 0.8 copy-start.5
